TPU v7x, 32 devices: a whole 2x2x4 slice. The times are simulated.
32 devices in a mesh: group: 2 (over x), src: 16 (over z, y, core).
Axes of the slice: x: 2, y: 2, z: 4, core: 2. Of those that a mesh axis runs over, the one named last changes fastest.
Arguments:
- positions: float32 [2, 32768], P(None, ('group', 'src')), parts along dimension 1, may hold values from -0.2 to 0.2
- flux: float32 [4, 32768], P(None, ('group', 'src')), parts along dimension 1, may hold values from 0.1 to 2
- cluster: int32 [32768], P(('group', 'src')), parts along dimension 0, may hold values from 0 to 15
- jones: float32 [4, 2, 16, 1024], P(None, None, None, ('group', 'src')), parts along dimension 3, may hold values from -4 to 4
- station_uvw: float32 [3, 1024], P(None, ('group', 'src')), parts along dimension 1, may hold values from -600 to 600
- channels: int32 [8], P('group'), parts along dimension 0, may hold values from 0 to 383
- tile_map: int32 [32, 2], P('group'), parts along dimension 0, may hold values from 0 to 15, as said below
Outputs:
- visibilities: float32 [32, 4, 2, 1024], P(('group', 'src')), parts along dimension 0
There are 2 independent parts, one for each index of `group`. A program takes and returns all parts, laid end to end along the dimension named above; each array names one. Nothing has to cross between parts.
Inputs may be any that keep to these rules, and one draw needn't show every extreme that they name: `tile_map`: each row is a pair of station tiles (first, second) with first <= second; the 16 pairs are distinct.
All inputs are finite; a program needn't handle non-finite values.
Results may differ from a plain program's by a relative error of at most 0.0038.
Values sent between devices are 32-bit elements; how exact they have to be, the bound alone decides.
No kernel may reach another device: no remote copies, remote signals or barrier semaphores. Data moves between devices by JAX's collectives and lax.ppermute only.
A program may use at most 128 MiB of HBM per device.

v0:
```python
import math

import jax
import jax.numpy as jnp
from jax import lax
from jax.sharding import PartitionSpec as P

S = 512
TS = 32


def phasors(station_gain, coords_uvw, coords, cluster_val, freq_ratio):
    directions = station_gain.shape[2]
    onehot = (cluster_val[None, :] == jnp.arange(directions, dtype=jnp.float32)[:, None]).astype(
        jnp.float32
    )
    gain_re = jnp.einsum("ckp,kn->cpn", station_gain[:, 0], onehot, precision=lax.Precision.HIGHEST)
    gain_im = jnp.einsum("ckp,kn->cpn", station_gain[:, 1], onehot, precision=lax.Precision.HIGHEST)
    l_term = coords[0]
    m_term = coords[1]
    n_term = jnp.sqrt(1.0 - l_term * l_term - m_term * m_term)
    argument = (
        coords_uvw[0][:, None] * l_term[None, :]
        + coords_uvw[1][:, None] * m_term[None, :]
        + coords_uvw[2][:, None] * (n_term - 1.0)[None, :]
    )
    phase = (2.0 * math.pi * freq_ratio)[:, None, None] * argument[None]
    cosine = jnp.cos(phase)
    sine = jnp.sin(phase)
    real_part = gain_re * cosine + gain_im * sine
    imag_part = gain_im * cosine - gain_re * sine
    return (real_part, imag_part)


def weighted_side(real_part, imag_part, fluxes, scale):
    weight = fluxes[:, None, :] * scale
    return jnp.stack([real_part * weight, imag_part * weight], 2).astype(jnp.bfloat16)


def plain_side(real_part, imag_part):
    return jnp.stack([real_part, imag_part], 2).astype(jnp.bfloat16)


def tile_products(left_sel, right_sel):
    real_sum = jnp.einsum(
        "cgirx,cgjrx->gcij", left_sel, right_sel, preferred_element_type=jnp.float32
    )
    imag_sum = jnp.einsum(
        "cgix,cgjx->gcij",
        left_sel[:, :, :, 1],
        right_sel[:, :, :, 0],
        preferred_element_type=jnp.float32,
    ) - jnp.einsum(
        "cgix,cgjx->gcij",
        left_sel[:, :, :, 0],
        right_sel[:, :, :, 1],
        preferred_element_type=jnp.float32,
    )
    return jnp.stack([real_sum, imag_sum], 2)


def clear_autos(values, pairs):
    same_tile = (pairs[:, 0] == pairs[:, 1])[:, None, None, None, None]
    diagonal = (jnp.arange(TS)[:, None] == jnp.arange(TS)[None, :])[None, None, None]
    return jnp.where(same_tile & diagonal, jnp.float32(0.0), values)


def select_stations(jones_all, uvw_all, pairs):
    chans = jones_all.shape[0]
    directions = jones_all.shape[2]
    tiles = S // TS
    count = pairs.shape[0]
    jones_tiles = jones_all.reshape(chans, 2, directions, tiles, TS)
    uvw_tiles = uvw_all.reshape(3, tiles, TS)
    first_gain = jnp.take(jones_tiles, pairs[:, 0], axis=3).reshape(
        chans, 2, directions, count * TS
    )
    second_gain = jnp.take(jones_tiles, pairs[:, 1], axis=3).reshape(
        chans, 2, directions, count * TS
    )
    first_uvw = jnp.take(uvw_tiles, pairs[:, 0], axis=1).reshape(3, count * TS)
    second_uvw = jnp.take(uvw_tiles, pairs[:, 1], axis=1).reshape(3, count * TS)
    return (first_gain, second_gain, first_uvw, second_uvw)


def add_tiles(carry, piece, stations, freq_ratio, scale, count):
    first_gain, second_gain, first_uvw, second_uvw = stations
    chans = first_gain.shape[0]
    length = piece.shape[1]
    width = math.gcd(length, 4096)

    def inner(turn, total):
        section = lax.dynamic_slice_in_dim(piece, turn * width, width, 1)
        coords = section[0:2]
        fluxes = section[2 : 2 + chans]
        kinds = section[2 + chans]
        first_re, first_im = phasors(first_gain, first_uvw, coords, kinds, freq_ratio)
        second_re, second_im = phasors(second_gain, second_uvw, coords, kinds, freq_ratio)
        left_sel = weighted_side(first_re, first_im, fluxes, scale).reshape(
            chans, count, TS, 2, width
        )
        right_sel = plain_side(second_re, second_im).reshape(chans, count, TS, 2, width)
        return total + tile_products(left_sel, right_sel)

    return lax.fori_loop(0, length // width, inner, carry)


def on_device(positions, flux, cluster, jones, station_uvw, channels, tile_map):
    freq_ratio = 1.0 + 0.002 * channels.astype(jnp.float32)
    src_dev = positions.shape[1]
    devices_src = lax.axis_size("src")
    scale = 1.0 / math.sqrt(src_dev * devices_src)
    chans = jones.shape[0]
    jones_all, uvw_all = (
        lax.all_gather(jones, "src", axis=3, tiled=True),
        lax.all_gather(station_uvw, "src", axis=1, tiled=True),
    )
    cluster_val = cluster.astype(jnp.float32)
    own_rows = tile_map.shape[0] // devices_src
    my_index = lax.axis_index("src")
    own_pairs = lax.dynamic_slice_in_dim(tile_map, my_index * own_rows, own_rows, 0)
    stations = select_stations(jones_all, uvw_all, own_pairs)
    source_rows = jnp.concatenate([positions, flux, cluster_val[None, :]], 0)
    start_total = jnp.zeros((own_rows, chans, 2, TS, TS), jnp.float32)
    total = add_tiles(
        start_total,
        lax.all_gather(source_rows, "src", axis=1, tiled=True),
        stations,
        freq_ratio,
        scale,
        own_rows,
    )
    return clear_autos(total, own_pairs).reshape(own_rows, chans, 2, TS * TS)


def solution(mesh):
    in_specs = (
        P(None, ("group", "src")),
        P(None, ("group", "src")),
        P(("group", "src")),
        P(None, None, None, ("group", "src")),
        P(None, ("group", "src")),
        P("group"),
        P("group", None),
    )
    out_specs = P(("group", "src"), None, None, None)
    return jax.shard_map(
        on_device, mesh=mesh, in_specs=in_specs, out_specs=out_specs, check_vma=False
    )
```

profile of v0, /device:TPU:1, one launch (start us, length us, event | category | flops | bytes accessed | tf_op | source)
XLA Modules:
  0.0 194.6 jit_solution(2198277265878676772)
XLA Ops:
  6.1 32.1 %all_gather.10 = f32[4,2,16,512]{2,0,1,3:T(4,128)S(1)} all-gather(f32[4,2,16,32]{2,0,1,3:T(4,128)S(1)} %copy.17), channel_id=1, replica_groups=mesh['group'=2,'src'=16] {'src'}, dimensions={3}, use_global_device_ids=true | all-gather | bytes 278528 | tf_op jit(solution)/shard_map/all_gather | solution.py:115
  38.6 20.1 %all-gather = f32[16,32,3]{1,2,0:T(4,128)S(1)} all-gather(f32[1,32,3]{1,2,0:T(4,128)S(1)} %bitcast.161), channel_id=1, replica_groups=mesh['group'=2,'src'=16] {'src'}, dimensions={0}, use_global_device_ids=true | all-gather | bytes 6528 | tf_op jit(solution)/shard_map/all_gather | solution.py:116
  59.0 20.3 %all_gather.9 = f32[7,16384]{1,0:T(8,128)} all-gather(f32[7,1024]{1,0:T(8,128)S(1)} %pad_maximum_fusion), channel_id=1, replica_groups=mesh['group'=2,'src'=16] {'src'}, dimensions={1}, use_global_device_ids=true | all-gather | bytes 487424 | tf_op jit(solution)/shard_map/all_gather | solution.py:127
  79.2 113.3 %while.18 = (s32[]{:T(128)}, f32[1,4,2,32,32]{4,3,1,2,0:T(8,128)S(1)}, f32[7,16384]{1,0:T(8,128)}, f32[4,2,16,32]{3,2,0,1:T(8,128)S(1)}, f32[4]{0:T(128)S(1)}, /...) while((s32[]{:T(128)}, ...), condition=%wide.region_1.0_spmd.clone, body=%wide.region_0.3_spmd.clone.sunk | while | flops 551092224 | bytes 27986972 | solution.py:105
  79.3 1.2 sqrt_add_fusion.2
  80.7 1.0 convolution_bitcast_fusion.7
  81.8 2.4 %convolution_bitcast_fusion.8 = f32[4,32,4096]{2,1,0:T(8,128)} fusion(f32[4096]{0:T(1024)S(1)} %bitcast.150, f32[4,2,16,32]{3,2,0,1:T(8,128)S(1)} %get-tuple-element.430), kind=kOutput, calls=%fused_computation.3.clone.1 | convolution fusion | flops 100728832 | bytes 2146304 | tf_op jit(solution)/shard_map/while/body/eval_jaxpr/ckp,kn->cpn/dot_general | solution.py:17
  84.1 2.3 %convolution_bitcast_fusion.9 = f32[4,32,4096]{2,1,0:T(8,128)} fusion(f32[4096]{0:T(1024)S(1)} %bitcast.151, f32[4,2,16,32]{3,2,0,1:T(8,128)S(1)} %get-tuple-element.430), kind=kOutput, calls=%fused_computation.2.clone.1 | convolution fusion | flops 100728832 | bytes 2146304 | tf_op jit(solution)/shard_map/while/body/eval_jaxpr/ckp,kn->cpn/dot_general | solution.py:18
  87.5 18.3 %fusion.84 = (bf16[4,32,4096]{2,1,0:T(8,128)(2,1)S(1)}, bf16[4,32,4096]{2,1,0:T(8,128)(2,1)S(1)}, bf16[4,32,4096]{2,1,0:T(8,128)(2,1)S(1)}, bf16[4,32,4096]{2,1,0:T(8,128)(2,1)S(1)}) fusion(f32[4,32,4096]{2,1,0:T(8,128)S(1)} %convolution_bitcast_fusion.7, f32[32,4096]{1,0:T(8,128)S(1)} %get-tuple-element.391, f32[4]{0:T(128)S(1)} %broadcast_multiply_fusion.2, ...), kind=kOutput, calls=%fused_computation.19.clone.1 | convolution fusion | flops 111214592 | bytes 11649536 | tf_op jit(solution)/shard_map/while/body/eval_jaxpr/ckp,kn->cpn/dot_general | solution.py:17
  107.6 1.2 sqrt_add_fusion.2
  109.0 1.0 convolution_bitcast_fusion.7
  110.1 2.4 %convolution_bitcast_fusion.8 = f32[4,32,4096]{2,1,0:T(8,128)} fusion(f32[4096]{0:T(1024)S(1)} %bitcast.150, f32[4,2,16,32]{3,2,0,1:T(8,128)S(1)} %get-tuple-element.430), kind=kOutput, calls=%fused_computation.3.clone.1 | convolution fusion | flops 100728832 | bytes 2146304 | tf_op jit(solution)/shard_map/while/body/eval_jaxpr/ckp,kn->cpn/dot_general | solution.py:17
  112.4 2.3 %convolution_bitcast_fusion.9 = f32[4,32,4096]{2,1,0:T(8,128)} fusion(f32[4096]{0:T(1024)S(1)} %bitcast.151, f32[4,2,16,32]{3,2,0,1:T(8,128)S(1)} %get-tuple-element.430), kind=kOutput, calls=%fused_computation.2.clone.1 | convolution fusion | flops 100728832 | bytes 2146304 | tf_op jit(solution)/shard_map/while/body/eval_jaxpr/ckp,kn->cpn/dot_general | solution.py:18
  115.8 18.3 %fusion.84 = (bf16[4,32,4096]{2,1,0:T(8,128)(2,1)S(1)}, bf16[4,32,4096]{2,1,0:T(8,128)(2,1)S(1)}, bf16[4,32,4096]{2,1,0:T(8,128)(2,1)S(1)}, bf16[4,32,4096]{2,1,0:T(8,128)(2,1)S(1)}) fusion(f32[4,32,4096]{2,1,0:T(8,128)S(1)} %convolution_bitcast_fusion.7, f32[32,4096]{1,0:T(8,128)S(1)} %get-tuple-element.391, f32[4]{0:T(128)S(1)} %broadcast_multiply_fusion.2, ...), kind=kOutput, calls=%fused_computation.19.clone.1 | convolution fusion | flops 111214592 | bytes 11649536 | tf_op jit(solution)/shard_map/while/body/eval_jaxpr/ckp,kn->cpn/dot_general | solution.py:17
  135.9 1.2 sqrt_add_fusion.2
  137.4 1.0 convolution_bitcast_fusion.7
  138.4 2.4 %convolution_bitcast_fusion.8 = f32[4,32,4096]{2,1,0:T(8,128)} fusion(f32[4096]{0:T(1024)S(1)} %bitcast.150, f32[4,2,16,32]{3,2,0,1:T(8,128)S(1)} %get-tuple-element.430), kind=kOutput, calls=%fused_computation.3.clone.1 | convolution fusion | flops 100728832 | bytes 2146304 | tf_op jit(solution)/shard_map/while/body/eval_jaxpr/ckp,kn->cpn/dot_general | solution.py:17
  140.8 2.3 %convolution_bitcast_fusion.9 = f32[4,32,4096]{2,1,0:T(8,128)} fusion(f32[4096]{0:T(1024)S(1)} %bitcast.151, f32[4,2,16,32]{3,2,0,1:T(8,128)S(1)} %get-tuple-element.430), kind=kOutput, calls=%fused_computation.2.clone.1 | convolution fusion | flops 100728832 | bytes 2146304 | tf_op jit(solution)/shard_map/while/body/eval_jaxpr/ckp,kn->cpn/dot_general | solution.py:18
  144.1 18.3 %fusion.84 = (bf16[4,32,4096]{2,1,0:T(8,128)(2,1)S(1)}, bf16[4,32,4096]{2,1,0:T(8,128)(2,1)S(1)}, bf16[4,32,4096]{2,1,0:T(8,128)(2,1)S(1)}, bf16[4,32,4096]{2,1,0:T(8,128)(2,1)S(1)}) fusion(f32[4,32,4096]{2,1,0:T(8,128)S(1)} %convolution_bitcast_fusion.7, f32[32,4096]{1,0:T(8,128)S(1)} %get-tuple-element.391, f32[4]{0:T(128)S(1)} %broadcast_multiply_fusion.2, ...), kind=kOutput, calls=%fused_computation.19.clone.1 | convolution fusion | flops 111214592 | bytes 11649536 | tf_op jit(solution)/shard_map/while/body/eval_jaxpr/ckp,kn->cpn/dot_general | solution.py:17
  164.2 1.2 sqrt_add_fusion.2
  165.7 1.0 convolution_bitcast_fusion.7
  166.7 2.4 %convolution_bitcast_fusion.8 = f32[4,32,4096]{2,1,0:T(8,128)} fusion(f32[4096]{0:T(1024)S(1)} %bitcast.150, f32[4,2,16,32]{3,2,0,1:T(8,128)S(1)} %get-tuple-element.430), kind=kOutput, calls=%fused_computation.3.clone.1 | convolution fusion | flops 100728832 | bytes 2146304 | tf_op jit(solution)/shard_map/while/body/eval_jaxpr/ckp,kn->cpn/dot_general | solution.py:17
  169.1 2.3 %convolution_bitcast_fusion.9 = f32[4,32,4096]{2,1,0:T(8,128)} fusion(f32[4096]{0:T(1024)S(1)} %bitcast.151, f32[4,2,16,32]{3,2,0,1:T(8,128)S(1)} %get-tuple-element.430), kind=kOutput, calls=%fused_computation.2.clone.1 | convolution fusion | flops 100728832 | bytes 2146304 | tf_op jit(solution)/shard_map/while/body/eval_jaxpr/ckp,kn->cpn/dot_general | solution.py:18
  172.5 18.3 %fusion.84 = (bf16[4,32,4096]{2,1,0:T(8,128)(2,1)S(1)}, bf16[4,32,4096]{2,1,0:T(8,128)(2,1)S(1)}, bf16[4,32,4096]{2,1,0:T(8,128)(2,1)S(1)}, bf16[4,32,4096]{2,1,0:T(8,128)(2,1)S(1)}) fusion(f32[4,32,4096]{2,1,0:T(8,128)S(1)} %convolution_bitcast_fusion.7, f32[32,4096]{1,0:T(8,128)S(1)} %get-tuple-element.391, f32[4]{0:T(128)S(1)} %broadcast_multiply_fusion.2, ...), kind=kOutput, calls=%fused_computation.19.clone.1 | convolution fusion | flops 111214592 | bytes 11649536 | tf_op jit(solution)/shard_map/while/body/eval_jaxpr/ckp,kn->cpn/dot_general | solution.py:17
  (67 shorter events, 15.6 us)
Async XLA Ops:
  0.0 0.7 copy-start
  0.0 38.6 %copy-start.4 = (f32[3,32]{1,0:T(4,128)S(1)}, f32[3,32]{1,0:T(4,128)}, u32[]{:S(2)}) copy-start(f32[3,32]{1,0:T(4,128)} %param.17) | copy-start | bytes 1156
  0.0 58.9 %copy-start.3 = (s32[1024]{0:T(1024)S(1)}, s32[1024]{0:T(1024)}, u32[]{:S(2)}) copy-start(s32[1024]{0:T(1024)} %param.15) | copy-start | bytes 12292
  0.0 58.9 %copy-start.2 = (f32[2,1024]{1,0:T(2,128)S(1)}, f32[2,1024]{1,0:T(2,128)}, u32[]{:S(2)}) copy-start(f32[2,1024]{1,0:T(2,128)} %param.13) | copy-start | bytes 24580
  0.0 58.9 %copy-start.1 = (f32[4,1024]{1,0:T(4,128)S(1)}, f32[4,1024]{1,0:T(4,128)}, u32[]{:S(2)}) copy-start(f32[4,1024]{1,0:T(4,128)} %param.14) | copy-start | bytes 49156
  6.1 73.2 %copy-start.5 = (s32[4]{0:T(128)S(1)}, s32[4]{0:T(128)}, u32[]{:S(2)}) copy-start(s32[4]{0:T(128)} %param.18) | copy-start | bytes 52
where the time goes:
time: 195 us
  matrix products  103 us (53%)
  blocking collectives  72.5 us (37%)
  other arithmetic  10.1 us (5%)
  between operations  5.17 us (3%)
  local copies, waits for them, and re-layouts  3.48 us (2%)
    dot_general x8, matrix products, phasors(): jnp.einsum('ckp,kn->cpn', station_gain[:, 0], onehot, precision=lax.Preci...  82.7 us
    all_gather x1, blocking collectives, on_device(): lax.all_gather(jones, 'src', axis=3, tiled=True)  32.1 us
    all_gather x1, blocking collectives, on_device(): lax.all_gather(source_rows, 'src', axis=1, tiled=True)  20.3 us
    all_gather x1, blocking collectives, on_device(): lax.all_gather(station_uvw, 'src', axis=1, tiled=True)  20.1 us
    dot_general x8, matrix products, phasors(): jnp.einsum('ckp,kn->cpn', station_gain[:, 1], onehot, precision=lax.Preci...  13.5 us
    sub x4, other arithmetic, phasors(): n_term - 1.0  4.79 us
    mul x4, other arithmetic, weighted_side(): weight = fluxes[:, None, :] * scale  4 us

commit v1 on v0

v1 whole, which is shorter than its diff:
```python
import functools
import math

import jax
import jax.numpy as jnp
from jax import lax
from jax.experimental import pallas as pl
from jax.experimental.pallas import tpu as pltpu
from jax.sharding import PartitionSpec as P

TS = 32
LANES = 128

A0, A1, A2, A3 = 3.1415628696601985, -5.166617869525222, 2.538088675224665, -0.546492984410238
B0, B1, B2 = A0 / A3, A1 / A3, A2 / A3
TOP = 1.0 / (A3 * A3)
GUARD = TOP * (1.0 + 1e-6)
SCALE = 2.0 * A3 * A3

ROWS_K = 128
GAIN_AT = 48


def split3(x):
    a = x.astype(jnp.bfloat16).astype(jnp.float32)
    b = (x - a).astype(jnp.bfloat16).astype(jnp.float32)
    return a, b, x - a - b


def station_rows(block):
    coords = block[0:8]
    re = block[8:24]
    im = block[24:40]
    turns = jnp.arctan2(im, re) * (-0.5 / math.pi)
    big = jnp.maximum(jnp.abs(re), jnp.abs(im))
    small = jnp.minimum(jnp.abs(re), jnp.abs(im))
    ratio = small / jnp.where(big == 0.0, 1.0, big)
    size = SCALE * big * jnp.sqrt(1.0 + ratio * ratio)
    u0, u1, u2 = split3(coords)
    t0, t1, t2 = split3(turns)
    g0, g1, g2 = split3(size)
    pad = jnp.zeros((ROWS_K - GAIN_AT - 48, block.shape[1]), jnp.float32)
    none = jnp.zeros((GAIN_AT, block.shape[1]), jnp.float32)
    phase = jnp.concatenate([u0, u0, u1, u0, u2, u1, t0, t1, t2, pad], 0)
    amplitude = jnp.concatenate([none, g0, g1, g2, pad], 0)
    return phase.T.astype(jnp.bfloat16), amplitude.T.astype(jnp.bfloat16)


def source_rows(src):
    s0, s1, s2 = split3(src)
    kinds = lax.broadcasted_iota(jnp.int32, (16, src.shape[1]), 0).astype(jnp.float32)
    onehot = jnp.where(src[3:4] == kinds, 1.0, 0.0)
    return jnp.concatenate([s0, s1, s0, s2, s0, s1, onehot, onehot, onehot], 0)


def phasor(turns, size):
    r = turns - lax.round(turns, lax.RoundingMethod.TO_NEAREST_EVEN)
    y = r * r
    s = r * (((y + B2) * y + B1) * y + B0)
    q = s * s
    rest = GUARD - q
    c = rest * lax.rsqrt(rest)
    return size * (0.5 * TOP - q), (size * s) * c


def tile_kernel(chans, shards, width, step, st_count, so_count, *refs):
    at_ref = refs[0]
    st_pieces = refs[1 : 1 + st_count]
    so_pieces = refs[1 + st_count : 1 + st_count + so_count]
    out_ref, st_buf, so_buf, lhs, rows, sides, total, st_sem, so_sem = refs[1 + st_count + so_count :]
    copies = []
    for pieces, buf, sem in ((st_pieces, st_buf, st_sem), (so_pieces, so_buf, so_sem)):
        begin = 0
        for n, piece in enumerate(pieces):
            size = piece.shape[0]
            copy = pltpu.make_async_copy(piece, buf.at[pl.ds(begin, size)], sem.at[n])
            copy.start()
            copies.append(copy)
            begin += size
    total[...] = jnp.zeros_like(total)
    rows[96:, :] = jnp.zeros((ROWS_K - 96, width), jnp.bfloat16)
    for copy in copies:
        copy.wait()
    for side in range(2):
        phase, amplitude = station_rows(st_buf[at_ref[side]])
        lhs[side * LANES : (side + 1) * LANES] = phase
        lhs[(2 + side) * LANES : (3 + side) * LANES] = amplitude

    def shard(i, carry):
        src = so_buf[i]
        rows[0:96, :] = source_rows(src).astype(jnp.bfloat16)
        for j in range(width // step):
            cut = slice(j * step, (j + 1) * step)
            both = jnp.dot(lhs[...], rows[:, cut], preferred_element_type=jnp.float32)
            for side in range(2):
                for c in range(chans):
                    at = (side * chans + c) * TS
                    turns = both[at : at + TS]
                    size = both[2 * LANES + at : 2 * LANES + at + TS]
                    if side == 0:
                        size = size * src[4 + c : 5 + c, cut]
                    re, im = phasor(turns, size)
                    sides[2 * at : 2 * at + TS, cut] = re.astype(jnp.bfloat16)
                    sides[2 * at + TS : 2 * at + 2 * TS, cut] = im.astype(jnp.bfloat16)
        for c in range(chans):
            left = sides[2 * c * TS : 2 * (c + 1) * TS]
            right = sides[2 * (chans + c) * TS : 2 * (chans + c + 1) * TS]
            total[c] += lax.dot_general(
                left, right, (((1,), (1,)), ((), ())), preferred_element_type=jnp.float32
            )
        return carry

    lax.fori_loop(0, shards, shard, 0)
    same = at_ref[2] == 1
    diagonal = lax.broadcasted_iota(jnp.int32, (TS, TS), 0) == lax.broadcasted_iota(jnp.int32, (TS, TS), 1)
    clear = jnp.logical_and(diagonal, same)
    for c in range(chans):
        whole = total[c]
        real = whole[:TS, :TS] + whole[TS:, TS:]
        imag = whole[TS:, :TS] - whole[:TS, TS:]
        out_ref[c, 0] = jnp.where(clear, 0.0, real)
        out_ref[c, 1] = jnp.where(clear, 0.0, imag)


def predict(at, stations, sources, chans):
    shards = sum(s.shape[0] for s in sources)
    width = sources[0].shape[2]
    step = math.gcd(width, 256)
    held = sum(s.shape[0] for s in stations)
    kernel = functools.partial(tile_kernel, chans, shards, width, step, len(stations), len(sources))
    count = len(stations) + len(sources)
    return pl.pallas_call(
        kernel,
        out_shape=jax.ShapeDtypeStruct((chans, 2, TS, TS), jnp.float32),
        in_specs=[pl.BlockSpec(memory_space=pltpu.SMEM)] + [pl.BlockSpec(memory_space=pl.ANY)] * count,
        out_specs=pl.BlockSpec(memory_space=pltpu.VMEM),
        scratch_shapes=[
            pltpu.VMEM((held,) + stations[0].shape[1:], jnp.float32),
            pltpu.VMEM((shards,) + sources[0].shape[1:], jnp.float32),
            pltpu.VMEM((4 * LANES, ROWS_K), jnp.bfloat16),
            pltpu.VMEM((ROWS_K, width), jnp.bfloat16),
            pltpu.VMEM((4 * chans * TS, width), jnp.bfloat16),
            pltpu.VMEM((chans, 2 * TS, 2 * TS), jnp.float32),
            pltpu.SemaphoreType.DMA((len(stations),)),
            pltpu.SemaphoreType.DMA((len(sources),)),
        ],
        compiler_params=pltpu.CompilerParams(vmem_limit_bytes=32 << 20),
    )(at, *stations, *sources)


def spread(parts, size):
    held = [[x] for x in parts]
    bit = size // 2
    while bit:
        pairs = [(i, i ^ bit) for i in range(size)]
        sent = [x[0] if len(x) == 1 else jnp.concatenate(x, 0) for x in held]
        for x, whole in zip(held, sent):
            x.append(lax.ppermute(whole, "src", pairs))
        bit //= 2
    return held


def place(mask, size):
    at, order, bit = 0 * mask, 0, size // 2
    while bit:
        at = at + ((mask // bit) % 2) * (1 << order)
        order, bit = order + 1, bit // 2
    return at


def on_device(positions, flux, cluster, jones, station_uvw, channels, tile_map):
    size = lax.axis_size("src")
    src_dev = positions.shape[1]
    chans, _, directions, own = jones.shape
    scale = 1.0 / math.sqrt(src_dev * size)
    freq_ratio = 1.0 + 0.002 * channels.astype(jnp.float32)
    n_term = jnp.sqrt(1.0 - positions[0] * positions[0] - positions[1] * positions[1]) - 1.0
    source = jnp.concatenate(
        [positions, n_term[None], cluster.astype(jnp.float32)[None], flux * scale], 0
    )[None]
    coords = station_uvw[:, None, :] * freq_ratio[None, :, None]
    gains = jnp.transpose(jones, (1, 2, 0, 3))
    station = jnp.concatenate(
        [
            coords.reshape(3, chans * own),
            jnp.zeros((5, chans * own), jnp.float32),
            gains.reshape(2 * directions, chans * own),
        ],
        0,
    )[None]
    stations, sources = spread([station, source], size)
    me = lax.axis_index("src")
    own_rows = tile_map.shape[0] // size
    many = TS // own
    out = []
    for row in range(own_rows):
        pair = lax.dynamic_slice_in_dim(tile_map, me * own_rows + row, 1, 0)[0]
        same = (pair[0] == pair[1]).astype(jnp.int32)
        if many == 1:
            at = jnp.stack([place(pair[0] ^ me, size), place(pair[1] ^ me, size), same])
            used = stations
        else:
            whole = jnp.concatenate(stations, 0)
            of = place((pair[:, None] * many + jnp.arange(many)[None, :]) ^ me, size)
            picked = jnp.take(whole, of.reshape(-1), axis=0)
            picked = picked.reshape(2, many, whole.shape[1], chans, own)
            picked = jnp.transpose(picked, (0, 2, 3, 1, 4)).reshape(2, whole.shape[1], chans * TS)
            used = [picked]
            at = jnp.stack([0 * same, 0 * same + 1, same])
        out.append(predict(at, used, sources, chans))
    return jnp.stack(out).reshape(own_rows, chans, 2, TS * TS)


def solution(mesh):
    in_specs = (
        P(None, ("group", "src")),
        P(None, ("group", "src")),
        P(("group", "src")),
        P(None, None, None, ("group", "src")),
        P(None, ("group", "src")),
        P("group"),
        P("group", None),
    )
    out_specs = P(("group", "src"), None, None, None)
    return jax.shard_map(
        on_device, mesh=mesh, in_specs=in_specs, out_specs=out_specs, check_vma=False
    )
```

time: 195 us -> 44.5 us (0.23)
  matrix products: 103 us -> 0 us
  blocking collectives: 72.5 us -> 0 us
  Pallas kernels: 0 us -> 18.5 us
  starting transfers between devices: 0 us -> 13.7 us
  other arithmetic: 10.1 us -> 2.5 us
  waiting for transfers between devices: 0 us -> 3.66 us
  between operations: 5.17 us -> 2.7 us
    dot_general x28 -> x0, matrix products: 103 us -> none  [the longest x8 82.7 us: phasors(): jnp.einsum('ckp,kn->cpn', station_gain[:, 0], onehot, precision=lax.Preci...]
    all_gather x3 -> x0, blocking collectives: 72.5 us -> none  [the longest x1 32.1 us: on_device(): lax.all_gather(jones, 'src', axis=3, tiled=True)]
    pallas_call x0 -> x1, Pallas kernels: none -> 18.5 us  [predict(): pl.pallas_call(kernel, out_shape=jax.ShapeDtypeStruct((chans, 2, TS, TS),...]
    ppermute x0 -> x8, starting transfers between devices: none -> 13.7 us  [spread(): x.append(lax.ppermute(whole, 'src', pairs))]
    sub x4 -> x1, other arithmetic: 4.79 us -> 0.79 us  [on_device(): jnp.sqrt(1.0 - positions[0] * positions[0] - positions[1] * positions[1])]
    ppermute x0 -> x8, waiting for transfers between devices: none -> 3.66 us  [spread(): x.append(lax.ppermute(whole, 'src', pairs))]
    mul x8 -> x2, other arithmetic: 4.02 us -> 0.77 us  [the longest x1 0.76 us: on_device(): flux * scale]
  transfers between devices with their start and end apart: 0 -> 8, of which waited for: 0 -> 3; matrix products, arithmetic and copies ran while one was open for 0% -> 3% of each run, Pallas kernels for 0% -> 0%
where the time goes in v1:
time: 44.5 us; the launch traced here: 44 us
  Pallas kernels  18.5 us (42%)
  starting transfers between devices  13.7 us (31%)
  waiting for transfers between devices  3.66 us (8%)
  local copies, waits for them, and re-layouts  2.95 us (7%)
  between operations  2.7 us (6%)
  other arithmetic  2.5 us (6%)
    pallas_call x1, Pallas kernels, predict(): pl.pallas_call(kernel, out_shape=jax.ShapeDtypeStruct((chans, 2, TS, TS),...  18.5 us
    ppermute x8, starting transfers between devices, spread(): x.append(lax.ppermute(whole, 'src', pairs))  13.7 us
    ppermute x8, waiting for transfers between devices, spread(): x.append(lax.ppermute(whole, 'src', pairs))  3.66 us
    unnamed x10, local copies, waits for them, and re-layouts  1.16 us
  transfers between devices with their start and end apart: 8, of which 3 were waited for; matrix products, arithmetic and copies ran while one was open for 3% of the time, Pallas kernels for 0%

profile of v1, /device:TPU:1, one launch (start us, length us, event | category | flops | bytes accessed | tf_op | source)
XLA Modules:
  0.0 44.0 jit_solution(11721099160203151947)
XLA Ops:
  0.0 0.8 %broadcast_multiply_fusion = f32[4,1024]{1,0:T(4,128)S(1)} fusion(f32[4,1024]{1,0:T(4,128)} %param.8), kind=kLoop, calls=%fused_computation.8 | loop fusion | flops 4096 | bytes 32768 | tf_op jit(solution)/shard_map/mul | solution.py:179
  0.8 0.8 %sqrt_add_fusion = f32[1,1024]{1,0:T(1,128)S(1)} fusion(f32[2,1024]{1,0:T(2,128)} %param.7), kind=kLoop, calls=%fused_computation.9 | loop fusion | flops 5120 | bytes 12288 | tf_op jit(solution)/shard_map/sub | solution.py:177
  1.6 0.7 %maximum_bitcast_fusion.refs_6_ = f32[1,8,1024]{2,1,0:T(8,128)S(1)} fusion(f32[4,1024]{1,0:T(4,128)S(1)} %broadcast_multiply_fusion, f32[1,1024]{1,0:T(1,128)S(1)} %bitcast.14, f32[1,1024]{1,0:T(1,128)S(1)} %sqrt_add_fusion, f32[2,1024]{1,0:T(2,128)} %param.7), kind=kLoop, calls=%fused_computation.6 | loop fusion | flops 24576 | bytes 65536 | tf_op jit(solution)/shard_map/broadcast_in_dim | solution.py:178
  2.3 3.2 %collective-permute-start.4 = (f32[1,8,1024]{2,1,0:T(8,128)S(1)}, f32[1,8,1024]{2,1,0:T(8,128)S(1)}, u32[]{:S(2)}, u32[]{:S(2)}) collective-permute-start(f32[1,8,1024]{2,1,0:T(8,128)S(1)} %maximum_bitcast_fusion.refs_6_), channel_id=1, source_target_pairs={{0,8},{1,9},{2,10},{3,11},{4,12},{5,13},{6,14},{7,15},{8,0},{9,1},... | collective-permute-start | bytes 98312 | tf_op jit(solution)/shard_map/ppermute | solution.py:158
  5.6 0.1 reshape.12
  5.7 0.6 %copy-done.3 = f32[3,32]{1,0:T(4,128)S(1)} copy-done((f32[3,32]{1,0:T(4,128)S(1)}, f32[3,32]{1,0:T(4,128)}, u32[]{:S(2)}) %copy-start.3) | copy-done | bytes 408
  6.2 0.1 mul.62
  6.3 0.6 %copy-done.4 = s32[4]{0:T(128)S(1)} copy-done((s32[4]{0:T(128)S(1)}, s32[4]{0:T(128)}, u32[]{:S(2)}) %copy-start.4) | copy-done | bytes 40
  7.0 0.1 mul.65
  7.1 0.1 pad.23.clone
  7.1 0.1 maximum_bitcast_fusion.1.refs_1_
  7.3 1.4 %collective-permute-start.5 = (f32[2,8,1024]{2,1,0:T(8,128)S(1)}, f32[2,8,1024]{2,1,0:T(8,128)S(1)}, u32[]{:S(2)}, u32[]{:S(2)}) collective-permute-start(f32[2,8,1024]{2,1,0:T(8,128)S(1)} %pad_maximum_fusion.4), channel_id=1, source_target_pairs={{0,4},{1,5},{2,6},{3,7},{4,0},{5,1},{6,2},{7,3},{8,12},{9,13},{10,... | collective-permute-start | bytes 196616 | tf_op jit(solution)/shard_map/ppermute | solution.py:158
  8.7 2.1 %collective-permute-done.refs_2_ = f32[1,40,128]{2,1,0:T(8,128)S(1)} collective-permute-done((f32[1,40,128]{2,1,0:T(8,128)S(1)}, f32[1,40,128]{2,1,0:T(8,128)S(1)}, u32[]{:S(2)}, u32[]{:S(2)}) %collective-permute-start) | collective-permute-done | bytes 20512 | tf_op jit(solution)/shard_map/ppermute | solution.py:158
  10.8 1.3 %collective-permute-start.1 = (f32[2,40,128]{2,1,0:T(8,128)S(1)}, f32[2,40,128]{2,1,0:T(8,128)S(1)}, u32[]{:S(2)}, u32[]{:S(2)}) collective-permute-start(f32[2,40,128]{2,1,0:T(8,128)S(1)} %pad_maximum_fusion.5), channel_id=1, source_target_pairs={{0,4},{1,5},{2,6},{3,7},{4,0},{5,1},{6,2},{7,3},{8,12},{9,13},{10,... | collective-permute-start | bytes 122888 | tf_op jit(solution)/shard_map/ppermute | solution.py:158
  12.1 1.3 %collective-permute-start.6 = (f32[4,8,1024]{2,1,0:T(8,128)S(1)}, f32[4,8,1024]{2,1,0:T(8,128)S(1)}, u32[]{:S(2)}, u32[]{:S(2)}) collective-permute-start(f32[4,8,1024]{2,1,0:T(8,128)S(1)} %pad_maximum_fusion.2), channel_id=1, source_target_pairs={{0,2},{1,3},{2,0},{3,1},{4,6},{5,7},{6,4},{7,5},{8,10},{9,11},{10,... | collective-permute-start | bytes 393224 | tf_op jit(solution)/shard_map/ppermute | solution.py:158
  13.5 0.2 collective-permute-done.1.refs_3_
  13.6 1.2 %collective-permute-start.2 = (f32[4,40,128]{2,1,0:T(8,128)S(1)}, f32[4,40,128]{2,1,0:T(8,128)S(1)}, u32[]{:S(2)}, u32[]{:S(2)}) collective-permute-start(f32[4,40,128]{2,1,0:T(8,128)S(1)} %pad_maximum_fusion.3), channel_id=1, source_target_pairs={{0,2},{1,3},{2,0},{3,1},{4,6},{5,7},{6,4},{7,5},{8,10},{9,11},{10,... | collective-permute-start | bytes 245768 | tf_op jit(solution)/shard_map/ppermute | solution.py:158
  14.9 1.4 %collective-permute-done.6.refs_9_ = f32[4,8,1024]{2,1,0:T(8,128)S(1)} collective-permute-done((f32[4,8,1024]{2,1,0:T(8,128)S(1)}, f32[4,8,1024]{2,1,0:T(8,128)S(1)}, u32[]{:S(2)}, u32[]{:S(2)}) %collective-permute-start.6) | collective-permute-done | bytes 131104 | tf_op jit(solution)/shard_map/ppermute | solution.py:158
  16.3 3.4 %collective-permute-start.7 = (f32[8,8,1024]{2,1,0:T(8,128)S(1)}, f32[8,8,1024]{2,1,0:T(8,128)S(1)}, u32[]{:S(2)}, u32[]{:S(2)}) collective-permute-start(f32[8,8,1024]{2,1,0:T(8,128)S(1)} %pad_maximum_fusion), channel_id=1, source_target_pairs={{0,1},{1,0},{2,3},{3,2},{4,5},{5,4},{6,7},{7,6},{8,9},{9,8},{10,11... | collective-permute-start | bytes 786440 | tf_op jit(solution)/shard_map/ppermute | solution.py:158
  19.7 1.8 %collective-permute-start.3 = (f32[8,40,128]{2,1,0:T(8,128)S(1)}, f32[8,40,128]{2,1,0:T(8,128)S(1)}, u32[]{:S(2)}, u32[]{:S(2)}) collective-permute-start(f32[8,40,128]{2,1,0:T(8,128)S(1)} %pad_maximum_fusion.1), channel_id=1, source_target_pairs={{0,1},{1,0},{2,3},{3,2},{4,5},{5,4},{6,7},{7,6},{8,9},{9,8},{10,11... | collective-permute-start | bytes 491528 | tf_op jit(solution)/shard_map/ppermute | solution.py:158
  21.5 0.5 %fusion = (s32[1,1]{0,1:T(1,128)}, s32[1,1]{0,1:T(1,128)}) fusion(s32[1,2]{0,1:T(2,128)S(1)} %constant_dynamic-slice_fusion), kind=kLoop, calls=%fused_computation.14 | loop fusion | bytes 16 | tf_op jit(solution)/shard_map/slice | solution.py:200
  24.7 0.1 pad_add_fusion.refs_0_
  24.7 18.5 %shard_map.73 = f32[4,2,32,32]{3,2,1,0:T(8,128)S(1)} custom-call(s32[3]{0:T(128)S(1)} %pad_add_fusion.refs_0_, f32[1,40,128]{2,1,0:T(8,128)S(1)} %maximum_bitcast_fusion.1.refs_1_, f32[1,40,128]{2,1,0:T(8,128)S(1)} %collective-permute-done.refs_2_, f32[2,40,128]{2,1,0:T(8,128)S(1)} %collective-permute-done.1.refs_3_, ...), custom_call_target="tpu_custom_call" | custom-call | tf_op jit(solution)/shard_map/pallas_call | solution.py:132
  43.3 0.7 %reshape_stack.3 = f32[1,4,2,1024]{3,2,1,0:T(2,128)} reshape(f32[4,2,32,32]{3,2,1,0:T(8,128)S(1)} %shard_map.73) | data formatting | bytes 65536 | tf_op jit(solution)/shard_map/reshape;stack | solution.py:211
  (28 shorter events, 0.3 us)
Async XLA Ops:
  0.0 13.4 %copy-start = (s32[16,2]{0,1:T(2,128)S(1)}, s32[16,2]{0,1:T(2,128)}, u32[]{:S(2)}) copy-start(s32[16,2]{0,1:T(2,128)} %param.13) | copy-start | bytes 388
  0.0 0.8 %copy-start.2 = (s32[1024]{0:T(1024)S(1)}, s32[1024]{0:T(1024)}, u32[]{:S(2)}) copy-start(s32[1024]{0:T(1024)} %param.9) | copy-start | bytes 12292
  0.0 5.5 %copy-start.1 = (f32[4,2,16,32]{3,2,1,0:T(8,128)S(1)}, f32[4,2,16,32]{3,2,1,0:T(8,128)}, u32[]{:S(2)}) copy-start(f32[4,2,16,32]{3,2,1,0:T(8,128)} %param.10) | copy-start | bytes 49156
  2.3 5.0 %collective-permute-start.4 = (f32[1,8,1024]{2,1,0:T(8,128)S(1)}, f32[1,8,1024]{2,1,0:T(8,128)S(1)}, u32[]{:S(2)}, u32[]{:S(2)}) collective-permute-start(f32[1,8,1024]{2,1,0:T(8,128)S(1)} %maximum_bitcast_fusion.refs_6_), channel_id=1, source_target_pairs={{0,8},{1,9},{2,10},{3,11},{4,12},{5,13},{6,14},{7,15},{8,0},{9,1},... | collective-permute-start | bytes 98312 | tf_op jit(solution)/shard_map/ppermute | solution.py:158
  5.6 0.7 %copy-start.3 = (f32[3,32]{1,0:T(4,128)S(1)}, f32[3,32]{1,0:T(4,128)}, u32[]{:S(2)}) copy-start(f32[3,32]{1,0:T(4,128)} %param.11) | copy-start | bytes 1156
  6.2 0.7 %copy-start.4 = (s32[4]{0:T(128)S(1)}, s32[4]{0:T(128)}, u32[]{:S(2)}) copy-start(s32[4]{0:T(128)} %param.12) | copy-start | bytes 52
  7.2 3.5 %collective-permute-start = (f32[1,40,128]{2,1,0:T(8,128)S(1)}, f32[1,40,128]{2,1,0:T(8,128)S(1)}, u32[]{:S(2)}, u32[]{:S(2)}) collective-permute-start(f32[1,40,128]{2,1,0:T(8,128)S(1)} %maximum_bitcast_fusion.1.refs_1_), channel_id=1, source_target_pairs={{0,8},{1,9},{2,10},{3,11},{4,12},{5,13},{6,14},{7,15},{8,0},{9,1},... | collective-permute-start | bytes 61448 | tf_op jit(solution)/shard_map/ppermute | solution.py:158
  7.3 4.8 %collective-permute-start.5 = (f32[2,8,1024]{2,1,0:T(8,128)S(1)}, f32[2,8,1024]{2,1,0:T(8,128)S(1)}, u32[]{:S(2)}, u32[]{:S(2)}) collective-permute-start(f32[2,8,1024]{2,1,0:T(8,128)S(1)} %pad_maximum_fusion.4), channel_id=1, source_target_pairs={{0,4},{1,5},{2,6},{3,7},{4,0},{5,1},{6,2},{7,3},{8,12},{9,13},{10,... | collective-permute-start | bytes 196616 | tf_op jit(solution)/shard_map/ppermute | solution.py:158
  10.8 2.9 %collective-permute-start.1 = (f32[2,40,128]{2,1,0:T(8,128)S(1)}, f32[2,40,128]{2,1,0:T(8,128)S(1)}, u32[]{:S(2)}, u32[]{:S(2)}) collective-permute-start(f32[2,40,128]{2,1,0:T(8,128)S(1)} %pad_maximum_fusion.5), channel_id=1, source_target_pairs={{0,4},{1,5},{2,6},{3,7},{4,0},{5,1},{6,2},{7,3},{8,12},{9,13},{10,... | collective-permute-start | bytes 122888 | tf_op jit(solution)/shard_map/ppermute | solution.py:158
  12.1 4.2 %collective-permute-start.6 = (f32[4,8,1024]{2,1,0:T(8,128)S(1)}, f32[4,8,1024]{2,1,0:T(8,128)S(1)}, u32[]{:S(2)}, u32[]{:S(2)}) collective-permute-start(f32[4,8,1024]{2,1,0:T(8,128)S(1)} %pad_maximum_fusion.2), channel_id=1, source_target_pairs={{0,2},{1,3},{2,0},{3,1},{4,6},{5,7},{6,4},{7,5},{8,10},{9,11},{10,... | collective-permute-start | bytes 393224 | tf_op jit(solution)/shard_map/ppermute | solution.py:158
  13.6 6.0 %collective-permute-start.2 = (f32[4,40,128]{2,1,0:T(8,128)S(1)}, f32[4,40,128]{2,1,0:T(8,128)S(1)}, u32[]{:S(2)}, u32[]{:S(2)}) collective-permute-start(f32[4,40,128]{2,1,0:T(8,128)S(1)} %pad_maximum_fusion.3), channel_id=1, source_target_pairs={{0,2},{1,3},{2,0},{3,1},{4,6},{5,7},{6,4},{7,5},{8,10},{9,11},{10,... | collective-permute-start | bytes 245768 | tf_op jit(solution)/shard_map/ppermute | solution.py:158
  16.3 8.5 %collective-permute-start.7 = (f32[8,8,1024]{2,1,0:T(8,128)S(1)}, f32[8,8,1024]{2,1,0:T(8,128)S(1)}, u32[]{:S(2)}, u32[]{:S(2)}) collective-permute-start(f32[8,8,1024]{2,1,0:T(8,128)S(1)} %pad_maximum_fusion), channel_id=1, source_target_pairs={{0,1},{1,0},{2,3},{3,2},{4,5},{5,4},{6,7},{7,6},{8,9},{9,8},{10,11... | collective-permute-start | bytes 786440 | tf_op jit(solution)/shard_map/ppermute | solution.py:158
  19.7 5.0 %collective-permute-start.3 = (f32[8,40,128]{2,1,0:T(8,128)S(1)}, f32[8,40,128]{2,1,0:T(8,128)S(1)}, u32[]{:S(2)}, u32[]{:S(2)}) collective-permute-start(f32[8,40,128]{2,1,0:T(8,128)S(1)} %pad_maximum_fusion.1), channel_id=1, source_target_pairs={{0,1},{1,0},{2,3},{3,2},{4,5},{5,4},{6,7},{7,6},{8,9},{9,8},{10,11... | collective-permute-start | bytes 491528 | tf_op jit(solution)/shard_map/ppermute | solution.py:158

commit v2 on v1

v2 whole, which is shorter than its diff:
```python
import functools
import math

import jax
import jax.numpy as jnp
from jax import lax
from jax.experimental import pallas as pl
from jax.experimental.pallas import tpu as pltpu
from jax.sharding import PartitionSpec as P

TS = 32
LANES = 128
STEP = 256

A0, A1, A2, A3 = 3.1415628696601985, -5.166617869525222, 2.538088675224665, -0.546492984410238
B0, B1, B2 = A0 / A3, A1 / A3, A2 / A3
TOP = 1.0 / (A3 * A3)
GUARD = TOP * (1.0 + 1e-6)
SCALE = 2.0 * A3 * A3

COORD_ROWS = 8
SOURCE_ROWS = 6 * COORD_ROWS


def split3(x):
    a = x.astype(jnp.bfloat16).astype(jnp.float32)
    b = (x - a).astype(jnp.bfloat16).astype(jnp.float32)
    return a, b, x - a - b


def station_rows(block, directions, depth):
    coords = block[:COORD_ROWS]
    re = block[COORD_ROWS : COORD_ROWS + directions]
    im = block[COORD_ROWS + directions :]
    turns = jnp.arctan2(im, re) * (-0.5 / math.pi)
    big = jnp.maximum(jnp.abs(re), jnp.abs(im))
    small = jnp.minimum(jnp.abs(re), jnp.abs(im))
    ratio = small / jnp.where(big == 0.0, 1.0, big)
    size = SCALE * big * jnp.sqrt(1.0 + ratio * ratio)
    u0, u1, u2 = split3(coords)
    t0, t1, t2 = split3(turns)
    g0, g1, g2 = split3(size)
    pad = jnp.zeros((depth - SOURCE_ROWS - 3 * directions, block.shape[1]), jnp.float32)
    none = jnp.zeros((SOURCE_ROWS, block.shape[1]), jnp.float32)
    phase = jnp.concatenate([u0, u0, u1, u0, u2, u1, t0, t1, t2, pad], 0)
    amplitude = jnp.concatenate([none, g0, g1, g2, pad], 0)
    return phase.T.astype(jnp.bfloat16), amplitude.T.astype(jnp.bfloat16)


def source_rows(src, directions, depth):
    s0, s1, s2 = split3(src)
    kinds = lax.broadcasted_iota(jnp.int32, (directions, src.shape[1]), 0).astype(jnp.float32)
    onehot = jnp.where(src[3:4] == kinds, 1.0, 0.0).astype(jnp.bfloat16)
    first = jnp.concatenate([s0, s1], 0).astype(jnp.bfloat16)
    second = jnp.concatenate([s0, s2], 0).astype(jnp.bfloat16)
    pad = jnp.zeros((depth - SOURCE_ROWS - 3 * directions, src.shape[1]), jnp.bfloat16)
    return jnp.concatenate([first, second, first, onehot, onehot, onehot, pad], 0)


def phasor(turns, size):
    r = turns - lax.round(turns, lax.RoundingMethod.TO_NEAREST_EVEN)
    y = r * r
    s = r * (((y + B2) * y + B1) * y + B0)
    q = s * s
    rest = GUARD - q
    c = rest * lax.rsqrt(rest)
    return size * (0.5 * TOP - q), (size * s) * c


def place(mask, size):
    at, order, bit = 0 * mask, 0, size // 2
    while bit:
        at = at + ((mask // bit) % 2) * (1 << order)
        order, bit = order + 1, bit // 2
    return at


def add_sources(chans, directions, depth, so_ref, lhs, total, both0, both1, sides0, sides1):
    shards, _, width = so_ref.shape
    step = math.gcd(width, STEP)
    per = width // step
    last = shards * per // 2
    sides1[...] = jnp.zeros_like(sides1)

    def part(t):
        return so_ref[t // per, :, pl.ds(pl.multiple_of(lax.rem(t, per) * step, step), step)]

    def product(t, into):
        made = source_rows(part(t), directions, depth)
        into[...] = jnp.dot(lhs[...], made, preferred_element_type=jnp.float32)

    def phasors(t, both, sides):
        weights = part(t)[4:]
        for side in range(2):
            for c in range(chans):
                at = (side * chans + c) * TS
                turns = both[at : at + TS]
                size = both[2 * LANES + at : 2 * LANES + at + TS]
                if side == 0:
                    size = size * weights[c : c + 1]
                re, im = phasor(turns, size)
                sides[2 * at : 2 * at + TS] = re.astype(jnp.bfloat16)
                sides[2 * at + TS : 2 * at + 2 * TS] = im.astype(jnp.bfloat16)

    def collect(sides):
        for at in range(0, 2 * chans * TS, LANES):
            total[at : at + LANES] += lax.dot_general(
                sides[at : at + LANES],
                sides[2 * chans * TS + at : 2 * chans * TS + at + LANES],
                (((1,), (1,)), ((), ())),
                preferred_element_type=jnp.float32,
            )

    product(0, both0)

    def turn(t, carry):
        product(last + t, both1)
        phasors(t, both0, sides0)
        collect(sides1)
        product(jnp.minimum(t + 1, last - 1), both0)
        phasors(last + t, both1, sides1)
        collect(sides0)
        return carry

    lax.fori_loop(0, last, turn, 0)
    collect(sides1)


def first_kernel(chans, directions, depth, row, size, pairs_ref, st0, st1, so_ref, lhs, total, *work):
    held = st0.shape[0]
    total[...] = jnp.zeros_like(total)
    for side in range(2):
        if row is None:
            at = side
        else:
            me = lax.axis_index("src")
            at = place(pairs_ref[me * row[0] + row[1], side] ^ me, size)
        low = lax.rem(at, held)
        block = jnp.where(at < held, st0[low], st1[low])
        phase, amplitude = station_rows(block, directions, depth)
        lhs[side * LANES : (side + 1) * LANES] = phase
        lhs[(2 + side) * LANES : (3 + side) * LANES] = amplitude
    add_sources(chans, directions, depth, so_ref, lhs, total, *work)


def next_kernel(chans, directions, depth, lhs, before, so_ref, total, *work):
    total[...] = before[...]
    add_sources(chans, directions, depth, so_ref, lhs, total, *work)


def last_kernel(chans, directions, depth, row, pairs_ref, lhs, before, so_ref, out_ref, total, *work):
    total[...] = before[...]
    add_sources(chans, directions, depth, so_ref, lhs, total, *work)
    me = lax.axis_index("src") * row[0] + row[1]
    same = pairs_ref[me, 0] == pairs_ref[me, 1]
    high = lax.broadcasted_iota(jnp.int32, (8, LANES), 0)
    lane = lax.broadcasted_iota(jnp.int32, (8, LANES), 1)
    fold = LANES // TS
    clear = jnp.logical_and(lane % TS == high * fold + lane // TS, same)
    for c in range(chans):
        base = 2 * c * TS
        column = base % LANES
        real = jnp.zeros((8, LANES), jnp.float32)
        imag = jnp.zeros((8, LANES), jnp.float32)
        for b in range(fold):
            w_re = total[pl.ds(base + b, 8, stride=fold)]
            w_im = total[pl.ds(base + TS + b, 8, stride=fold)]
            here = lane // TS == b
            one = (b * TS - column) % LANES
            two = (b * TS - column - TS) % LANES
            real = jnp.where(here, pltpu.roll(w_re, one, 1) + pltpu.roll(w_im, two, 1), real)
            imag = jnp.where(here, pltpu.roll(w_im, one, 1) - pltpu.roll(w_re, two, 1), imag)
        for n, values in enumerate((real, imag)):
            values = jnp.where(clear, 0.0, values)
            for m in range(8):
                out_ref[c, n : n + 1, m * LANES : (m + 1) * LANES] = values[m : m + 1]


class Predictor:
    def __init__(self, chans, directions, width):
        self.chans, self.directions = chans, directions
        self.depth = -(-(SOURCE_ROWS + 3 * directions) // LANES) * LANES
        step = math.gcd(width, STEP)
        self.work = [
            pltpu.VMEM((4 * LANES, step), jnp.float32),
            pltpu.VMEM((4 * LANES, step), jnp.float32),
            pltpu.VMEM((4 * chans * TS, step), jnp.bfloat16),
            pltpu.VMEM((4 * chans * TS, step), jnp.bfloat16),
        ]
        self.total = (2 * chans * TS, LANES)

    def call(self, kernel, out_shape, in_specs, scratch, args):
        vmem = pl.BlockSpec(memory_space=pltpu.VMEM)
        sources = args[-1].shape[0] * args[-1].shape[2]
        count = 2 * self.chans * TS * sources
        return pl.pallas_call(
            kernel,
            out_shape=out_shape,
            in_specs=in_specs + [vmem] * (len(args) - len(in_specs)),
            out_specs=jax.tree.map(lambda _: vmem, out_shape),
            scratch_shapes=scratch,
            compiler_params=pltpu.CompilerParams(vmem_limit_bytes=32 << 20),
            cost_estimate=pl.CostEstimate(flops=2000 * count, bytes_accessed=0, transcendentals=count),
        )(*args)

    def first(self, row, size, pairs, stations, sources):
        kernel = functools.partial(first_kernel, self.chans, self.directions, self.depth, row, size)
        shapes = (
            jax.ShapeDtypeStruct((4 * LANES, self.depth), jnp.bfloat16),
            jax.ShapeDtypeStruct(self.total, jnp.float32),
        )
        smem = pl.BlockSpec(memory_space=pltpu.SMEM)
        return self.call(kernel, shapes, [smem], self.work, (pairs, *stations, sources))

    def next(self, lhs, total, sources):
        kernel = functools.partial(next_kernel, self.chans, self.directions, self.depth)
        shape = jax.ShapeDtypeStruct(self.total, jnp.float32)
        return self.call(kernel, shape, [], self.work, (lhs, total, sources))

    def last(self, row, pairs, lhs, total, sources):
        kernel = functools.partial(last_kernel, self.chans, self.directions, self.depth, row)
        shape = jax.ShapeDtypeStruct((self.chans, 2, TS * TS), jnp.float32)
        smem = pl.BlockSpec(memory_space=pltpu.SMEM)
        scratch = [pltpu.VMEM(self.total, jnp.float32)] + self.work
        return self.call(kernel, shape, [smem], scratch, (pairs, lhs, total, sources))


def pack_kernel(scale, chans, channel_ref, positions_ref, flux_ref, cluster_ref, jones_ref, uvw_ref, station_ref, source_ref):
    own = uvw_ref.shape[1]
    directions = jones_ref.shape[2]
    coords = positions_ref[...]
    l_term, m_term = coords[0:1], coords[1:2]
    source_ref[0, 0:2] = coords
    source_ref[0, 2:3] = jnp.sqrt(1.0 - l_term * l_term - m_term * m_term) - 1.0
    source_ref[0, 3:4] = cluster_ref[...].astype(jnp.float32)
    source_ref[0, 4:] = flux_ref[...] * scale
    station_ref[...] = jnp.zeros_like(station_ref)
    for c in range(chans):
        lanes = slice(c * own, (c + 1) * own)
        ratio = 1.0 + 0.002 * channel_ref[c].astype(jnp.float32)
        station_ref[0, 0:3, lanes] = uvw_ref[...] * ratio
        for n in range(2):
            begin = COORD_ROWS + n * directions
            station_ref[0, begin : begin + directions, lanes] = jones_ref[c, n]


def pack(positions, flux, cluster, jones, station_uvw, channels, scale):
    chans, _, directions, own = jones.shape
    vmem = pl.BlockSpec(memory_space=pltpu.VMEM)
    return pl.pallas_call(
        functools.partial(pack_kernel, scale, chans),
        out_shape=(
            jax.ShapeDtypeStruct((1, COORD_ROWS + 2 * directions, chans * own), jnp.float32),
            jax.ShapeDtypeStruct((1, 4 + chans, positions.shape[1]), jnp.float32),
        ),
        in_specs=[pl.BlockSpec(memory_space=pltpu.SMEM)] + [vmem] * 5,
        out_specs=(vmem, vmem),
    )(channels, positions, flux, cluster[None], jones, station_uvw)


def swap(x, bit, size):
    return lax.ppermute(x, "src", [(i, i ^ bit) for i in range(size)])


def spread(station, size):
    bit = size // 2
    while bit:
        got = swap(station, bit, size)
        if bit > 1:
            station = jnp.concatenate([station, got], 0)
        bit //= 2
    return station, got


def on_device(positions, flux, cluster, jones, station_uvw, channels, tile_map):
    size = lax.axis_size("src")
    chans, _, directions, own = jones.shape
    scale = 1.0 / math.sqrt(positions.shape[1] * size)
    station, source = pack(positions, flux, cluster, jones, station_uvw, channels, scale)
    stations = spread(station, size)
    bit = size // 2
    while bit > 2:
        source = jnp.concatenate([source, swap(source, bit, size)], 0)
        bit //= 2
    own_rows = tile_map.shape[0] // size
    many = TS // own
    predictor = Predictor(chans, directions, positions.shape[1])
    begun = []
    for row in range(own_rows):
        if many == 1:
            begun.append(predictor.first((own_rows, row), size, tile_map, stations, source))
        else:
            me = lax.axis_index("src")
            pair = lax.dynamic_slice_in_dim(tile_map, me * own_rows + row, 1, 0)[0]
            whole = jnp.concatenate(stations, 0)
            of = place((pair[:, None] * many + jnp.arange(many)[None, :]) ^ me, size)
            picked = jnp.take(whole, of.reshape(-1), axis=0)
            picked = picked.reshape(2, many, whole.shape[1], chans, own)
            picked = jnp.transpose(picked, (0, 2, 3, 1, 4)).reshape(2, whole.shape[1], chans * TS)
            begun.append(predictor.first(None, size, tile_map, (picked, picked), source))
    got = swap(source, 2, size)
    both = jnp.concatenate([source, got], 0)
    other = swap(both, 1, size)
    out = []
    for row, (lhs, total) in enumerate(begun):
        total = predictor.next(lhs, total, got)
        out.append(predictor.last((own_rows, row), tile_map, lhs, total, other))
    return jnp.stack(out)


def solution(mesh):
    in_specs = (
        P(None, ("group", "src")),
        P(None, ("group", "src")),
        P(("group", "src")),
        P(None, None, None, ("group", "src")),
        P(None, ("group", "src")),
        P("group"),
        P("group", None),
    )
    out_specs = P(("group", "src"), None, None, None)
    return jax.shard_map(
        on_device, mesh=mesh, in_specs=in_specs, out_specs=out_specs, check_vma=False
    )
```

time: 44.5 us -> 38.7 us (0.87)
  between operations: 2.7 us -> 0.05 us
  other arithmetic: 2.5 us -> 0.04 us
  local copies, waits for them, and re-layouts: 2.95 us -> 0.91 us
  starting transfers between devices: 13.7 us -> 15.4 us
  waiting for transfers between devices: 3.66 us -> 2.27 us
  Pallas kernels: 18.5 us -> 19.8 us
    ppermute x8, starting transfers between devices: 13.7 us -> 15.4 us  [swap(): return lax.ppermute(x, 'src', [(i, i ^ bit) for i in range(size)])]
    ppermute x8, waiting for transfers between devices: 3.66 us -> 2.27 us  [swap(): return lax.ppermute(x, 'src', [(i, i ^ bit) for i in range(size)])]
    pallas_call x1 -> x4, Pallas kernels: 18.5 us -> 19.8 us  [the longest x3 18.3 us: call(): pl.pallas_call(kernel, out_shape=out_shape, in_specs=in_specs + [vmem] *...]
    broadcast_in_dim x2 -> x0, other arithmetic: 0.8 us -> none  [the longest x1 0.72 us: on_device(): jnp.concatenate([positions, n_term[None], cluster.astype(jnp.float32)[Non...]
    sub x1 -> x0, other arithmetic: 0.79 us -> none  [on_device(): jnp.sqrt(1.0 - positions[0] * positions[0] - positions[1] * positions[1])]
    mul x2 -> x0, other arithmetic: 0.77 us -> none  [the longest x1 0.76 us: on_device(): flux * scale]
    another operation x1 -> x0, local copies, waits for them, and re-layouts: 0.73 us -> none  [on_device(): return jnp.stack(out).reshape(own_rows, chans, 2, TS * TS)]
    slice x1 -> x0, local copies, waits for them, and re-layouts: 0.52 us -> none  [on_device(): at = jnp.stack([place(pair[0] ^ me, size), place(pair[1] ^ me, size), same])]
  transfers between devices with their start and end apart: 8 -> 8, of which waited for: 3 -> 3; matrix products, arithmetic and copies ran while one was open for 3% -> 2% of each run, Pallas kernels for 0% -> 23%
where the time goes in v2:
time: 38.7 us; the launch traced here: 38.4 us
  Pallas kernels  19.8 us (51%)
  starting transfers between devices  15.4 us (40%)
  waiting for transfers between devices  2.27 us (6%)
  local copies, waits for them, and re-layouts  0.91 us (2%)
    pallas_call x3, Pallas kernels, call(): pl.pallas_call(kernel, out_shape=out_shape, in_specs=in_specs + [vmem] *...  18.3 us
    ppermute x8, starting transfers between devices, swap(): return lax.ppermute(x, 'src', [(i, i ^ bit) for i in range(size)])  15.4 us
    ppermute x8, waiting for transfers between devices, swap(): return lax.ppermute(x, 'src', [(i, i ^ bit) for i in range(size)])  2.27 us
    pallas_call x1, Pallas kernels, pack(): pl.pallas_call(functools.partial(pack_kernel, scale, chans), out_shape=(j...  1.55 us
    unnamed x12, local copies, waits for them, and re-layouts  0.9 us
  transfers between devices with their start and end apart: 8, of which 3 were waited for; matrix products, arithmetic and copies ran while one was open for 2% of the time, Pallas kernels for 23%

profile of v2, /device:TPU:1, one launch (start us, length us, event | category | flops | bytes accessed | tf_op | source)
XLA Modules:
  0.0 38.4 jit_solution(4487465997676560213)
XLA Ops:
  0.0 1.5 %shard_map.73 = (f32[1,40,128]{2,1,0:T(8,128)}, f32[1,8,1024]{2,1,0:T(8,128)}) custom-call(s32[4]{0:T(128)} %channel_ref.1, f32[2,1024]{1,0:T(2,128)} %positions_ref.1, f32[4,1024]{1,0:T(4,128)} %flux_ref.1, s32[1,1024]{1,0:T(1,128)} %bitcast.2, f32[4,2,16,32]{3,2,1,0:T(8,128)} %jones_ref.1, f32[3,32]{1,0:T(4,128)} %uvw_ref.1), custom_call_target="tpu_custom_call" | custom-call | tf_op jit(solution)/shard_map/pallas_call | solution.py:250
  1.5 3.1 %collective-permute-start = (f32[1,40,128]{2,1,0:T(8,128)}, f32[1,40,128]{2,1,0:T(8,128)S(1)}, u32[]{:S(2)}, u32[]{:S(2)}) collective-permute-start(f32[1,40,128]{2,1,0:T(8,128)} %get-tuple-element.9), channel_id=1, source_target_pairs={{0,8},{1,9},{2,10},{3,11},{4,12},{5,13},{6,14},{7,15},{8,0},{9,1},... | collective-permute-start | bytes 61448 | tf_op jit(solution)/shard_map/ppermute | solution.py:262
  4.7 0.1 collective-permute-start.4
  4.8 0.8 %constant_dynamic-update-slice_fusion.6 = f32[4,8,1024]{2,1,0:T(8,128)S(1)} fusion(f32[1,8,1024]{2,1,0:T(8,128)} %get-tuple-element.10), kind=kLoop, calls=%fused_computation.10 | loop fusion | bytes 65536
  5.6 0.0 copy-done.1
  5.6 0.5 %collective-permute-done = f32[1,40,128]{2,1,0:T(8,128)S(1)} collective-permute-done((f32[1,40,128]{2,1,0:T(8,128)}, f32[1,40,128]{2,1,0:T(8,128)S(1)}, u32[]{:S(2)}, u32[]{:S(2)}) %collective-permute-start) | collective-permute-done | bytes 20512 | tf_op jit(solution)/shard_map/ppermute | solution.py:262
  6.1 1.4 %collective-permute-start.1 = (f32[2,40,128]{2,1,0:T(8,128)S(1)}, f32[2,40,128]{2,1,0:T(8,128)S(1)}, u32[]{:S(2)}, u32[]{:S(2)}) collective-permute-start(f32[2,40,128]{2,1,0:T(8,128)S(1)} %pad_maximum_fusion.3), channel_id=1, source_target_pairs={{0,4},{1,5},{2,6},{3,7},{4,0},{5,1},{6,2},{7,3},{8,12},{9,13},{10,... | collective-permute-start | bytes 122888 | tf_op jit(solution)/shard_map/ppermute | solution.py:262
  7.4 1.2 %collective-permute-done.4 = f32[1,8,1024]{2,1,0:T(8,128)S(1)} collective-permute-done((f32[1,8,1024]{2,1,0:T(8,128)}, f32[1,8,1024]{2,1,0:T(8,128)S(1)}, u32[]{:S(2)}, u32[]{:S(2)}) %collective-permute-start.4) | collective-permute-done | bytes 32800 | tf_op jit(solution)/shard_map/ppermute | solution.py:262
  8.6 1.3 %collective-permute-start.5 = (f32[2,8,1024]{2,1,0:T(8,128)S(1)}, f32[2,8,1024]{2,1,0:T(8,128)S(1)}, u32[]{:S(2)}, u32[]{:S(2)}) collective-permute-start(f32[2,8,1024]{2,1,0:T(8,128)S(1)} %pad_maximum_fusion.2), channel_id=1, source_target_pairs={{0,4},{1,5},{2,6},{3,7},{4,0},{5,1},{6,2},{7,3},{8,12},{9,13},{10,... | collective-permute-start | bytes 196616 | tf_op jit(solution)/shard_map/ppermute | solution.py:262
  9.9 0.0 collective-permute-done.1
  10.0 1.3 %collective-permute-start.2 = (f32[4,40,128]{2,1,0:T(8,128)S(1)}, f32[4,40,128]{2,1,0:T(8,128)S(1)}, u32[]{:S(2)}, u32[]{:S(2)}) collective-permute-start(f32[4,40,128]{2,1,0:T(8,128)S(1)} %pad_maximum_fusion.1), channel_id=1, source_target_pairs={{0,2},{1,3},{2,0},{3,1},{4,6},{5,7},{6,4},{7,5},{8,10},{9,11},{10,... | collective-permute-start | bytes 245768 | tf_op jit(solution)/shard_map/ppermute | solution.py:262
  11.3 0.6 %collective-permute-done.5 = f32[2,8,1024]{2,1,0:T(8,128)S(1)} collective-permute-done((f32[2,8,1024]{2,1,0:T(8,128)S(1)}, f32[2,8,1024]{2,1,0:T(8,128)S(1)}, u32[]{:S(2)}, u32[]{:S(2)}) %collective-permute-start.5) | collective-permute-done | bytes 65568 | tf_op jit(solution)/shard_map/ppermute | solution.py:262
  11.8 1.5 %collective-permute-start.6 = (f32[4,8,1024]{2,1,0:T(8,128)S(1)}, f32[4,8,1024]{2,1,0:T(8,128)S(1)}, u32[]{:S(2)}, u32[]{:S(2)}) collective-permute-start(f32[4,8,1024]{2,1,0:T(8,128)S(1)} %constant_dynamic-update-slice_fusion.4.so_ref), channel_id=1, source_target_pairs={{0,2},{1,3},{2,0},{3,1},{4,6},{5,7},{6,4},{7,5},{8,10},{9,11},{10,... | collective-permute-start | bytes 393224 | tf_op jit(solution)/shard_map/ppermute | solution.py:262
  13.4 0.0 collective-permute-done.2
  13.4 4.0 %collective-permute-start.3 = (f32[8,40,128]{2,1,0:T(8,128)S(1)}, f32[8,40,128]{2,1,0:T(8,128)S(1)}, u32[]{:S(2)}, u32[]{:S(2)}) collective-permute-start(f32[8,40,128]{2,1,0:T(8,128)S(1)} %constant_dynamic-update-slice_fusion.st0), channel_id=1, source_target_pairs={{0,1},{1,0},{2,3},{3,2},{4,5},{5,4},{6,7},{7,6},{8,9},{9,8},{10,11... | collective-permute-start | bytes 491528 | tf_op jit(solution)/shard_map/ppermute | solution.py:262
  17.4 0.0 copy-done.2
  17.4 0.1 copy.9.pairs_ref
  17.5 0.0 collective-permute-done.6.so_ref
  17.5 2.7 %collective-permute-start.7 = (f32[8,8,1024]{2,1,0:T(8,128)S(1)}, f32[8,8,1024]{2,1,0:T(8,128)S(1)}, u32[]{:S(2)}, u32[]{:S(2)}) collective-permute-start(f32[8,8,1024]{2,1,0:T(8,128)S(1)} %pad_maximum_fusion), channel_id=1, source_target_pairs={{0,1},{1,0},{2,3},{3,2},{4,5},{5,4},{6,7},{7,6},{8,9},{9,8},{10,11... | collective-permute-start | bytes 786440 | tf_op jit(solution)/shard_map/ppermute | solution.py:262
  20.1 0.0 collective-permute-done.3.st1
  20.1 4.9 %shard_map.74 = (bf16[512,128]{1,0:T(8,128)(2,1)S(1)}, f32[256,128]{1,0:T(8,128)S(1)}) custom-call(s32[16,2]{1,0:T(8,128)S(1)} %copy.9.pairs_ref, f32[8,40,128]{2,1,0:T(8,128)S(1)} %constant_dynamic-update-slice_fusion.st0, f32[8,40,128]{2,1,0:T(8,128)S(1)} %collective-permute-done.3.st1, f32[4,8,1024]{2,1,0:T(8,128)S(1)} %constant_dynamic-update-slice_fusion.4.so_ref), custom_call_target="tpu_custom_call" | custom-call | flops 2097152000 | tf_op jit(solution)/shard_map/pallas_call | solution.py:196
  25.0 4.1 %shard_map.75.before = f32[256,128]{1,0:T(8,128)S(1)} custom-call(bf16[512,128]{1,0:T(8,128)(2,1)S(1)} %get-tuple-element.11.lhs, f32[256,128]{1,0:T(8,128)S(1)} %get-tuple-element.12.before, f32[4,8,1024]{2,1,0:T(8,128)S(1)} %collective-permute-done.6.so_ref), custom_call_target="tpu_custom_call" | custom-call | flops 2097152000 | tf_op jit(solution)/shard_map/pallas_call | solution.py:196
  29.1 0.0 collective-permute-done.7.so_ref
  29.1 9.3 %shard_map.76 = f32[4,2,1024]{2,1,0:T(2,128)} custom-call(s32[16,2]{1,0:T(8,128)S(1)} %copy.9.pairs_ref, bf16[512,128]{1,0:T(8,128)(2,1)S(1)} %get-tuple-element.11.lhs, f32[256,128]{1,0:T(8,128)S(1)} %shard_map.75.before, f32[8,8,1024]{2,1,0:T(8,128)S(1)} %collective-permute-done.7.so_ref), custom_call_target="tpu_custom_call" | custom-call | flops 4194304000 | tf_op jit(solution)/shard_map/pallas_call | solution.py:196
  (14 shorter events, 0.1 us)
Async XLA Ops:
  1.5 4.5 %collective-permute-start = (f32[1,40,128]{2,1,0:T(8,128)}, f32[1,40,128]{2,1,0:T(8,128)S(1)}, u32[]{:S(2)}, u32[]{:S(2)}) collective-permute-start(f32[1,40,128]{2,1,0:T(8,128)} %get-tuple-element.9), channel_id=1, source_target_pairs={{0,8},{1,9},{2,10},{3,11},{4,12},{5,13},{6,14},{7,15},{8,0},{9,1},... | collective-permute-start | bytes 61448 | tf_op jit(solution)/shard_map/ppermute | solution.py:262
  4.7 0.9 %copy-start.1 = (f32[1,40,128]{2,1,0:T(8,128)S(1)}, f32[1,40,128]{2,1,0:T(8,128)}, u32[]{:S(2)}) copy-start(f32[1,40,128]{2,1,0:T(8,128)} %get-tuple-element.9) | copy-start | bytes 61444
  4.7 3.9 %collective-permute-start.4 = (f32[1,8,1024]{2,1,0:T(8,128)}, f32[1,8,1024]{2,1,0:T(8,128)S(1)}, u32[]{:S(2)}, u32[]{:S(2)}) collective-permute-start(f32[1,8,1024]{2,1,0:T(8,128)} %get-tuple-element.10), channel_id=1, source_target_pairs={{0,8},{1,9},{2,10},{3,11},{4,12},{5,13},{6,14},{7,15},{8,0},{9,1},... | collective-permute-start | bytes 98312 | tf_op jit(solution)/shard_map/ppermute | solution.py:262
  6.1 2.6 %copy-start = (f32[1,8,1024]{2,1,0:T(8,128)S(1)}, f32[1,8,1024]{2,1,0:T(8,128)}, u32[]{:S(2)}) copy-start(f32[1,8,1024]{2,1,0:T(8,128)} %get-tuple-element.10) | copy-start | bytes 98308
  6.1 3.9 %collective-permute-start.1 = (f32[2,40,128]{2,1,0:T(8,128)S(1)}, f32[2,40,128]{2,1,0:T(8,128)S(1)}, u32[]{:S(2)}, u32[]{:S(2)}) collective-permute-start(f32[2,40,128]{2,1,0:T(8,128)S(1)} %pad_maximum_fusion.3), channel_id=1, source_target_pairs={{0,4},{1,5},{2,6},{3,7},{4,0},{5,1},{6,2},{7,3},{8,12},{9,13},{10,... | collective-permute-start | bytes 122888 | tf_op jit(solution)/shard_map/ppermute | solution.py:262
  8.6 3.2 %collective-permute-start.5 = (f32[2,8,1024]{2,1,0:T(8,128)S(1)}, f32[2,8,1024]{2,1,0:T(8,128)S(1)}, u32[]{:S(2)}, u32[]{:S(2)}) collective-permute-start(f32[2,8,1024]{2,1,0:T(8,128)S(1)} %pad_maximum_fusion.2), channel_id=1, source_target_pairs={{0,4},{1,5},{2,6},{3,7},{4,0},{5,1},{6,2},{7,3},{8,12},{9,13},{10,... | collective-permute-start | bytes 196616 | tf_op jit(solution)/shard_map/ppermute | solution.py:262
  10.0 3.4 %collective-permute-start.2 = (f32[4,40,128]{2,1,0:T(8,128)S(1)}, f32[4,40,128]{2,1,0:T(8,128)S(1)}, u32[]{:S(2)}, u32[]{:S(2)}) collective-permute-start(f32[4,40,128]{2,1,0:T(8,128)S(1)} %pad_maximum_fusion.1), channel_id=1, source_target_pairs={{0,2},{1,3},{2,0},{3,1},{4,6},{5,7},{6,4},{7,5},{8,10},{9,11},{10,... | collective-permute-start | bytes 245768 | tf_op jit(solution)/shard_map/ppermute | solution.py:262
  11.8 5.5 %copy-start.2 = (s32[16,2]{0,1:T(2,128)S(1)}, s32[16,2]{0,1:T(2,128)}, u32[]{:S(2)}) copy-start(s32[16,2]{0,1:T(2,128)} %param.13) | copy-start | bytes 388
  11.8 5.6 %collective-permute-start.6 = (f32[4,8,1024]{2,1,0:T(8,128)S(1)}, f32[4,8,1024]{2,1,0:T(8,128)S(1)}, u32[]{:S(2)}, u32[]{:S(2)}) collective-permute-start(f32[4,8,1024]{2,1,0:T(8,128)S(1)} %constant_dynamic-update-slice_fusion.4.so_ref), channel_id=1, source_target_pairs={{0,2},{1,3},{2,0},{3,1},{4,6},{5,7},{6,4},{7,5},{8,10},{9,11},{10,... | collective-permute-start | bytes 393224 | tf_op jit(solution)/shard_map/ppermute | solution.py:262
  13.4 6.8 %collective-permute-start.3 = (f32[8,40,128]{2,1,0:T(8,128)S(1)}, f32[8,40,128]{2,1,0:T(8,128)S(1)}, u32[]{:S(2)}, u32[]{:S(2)}) collective-permute-start(f32[8,40,128]{2,1,0:T(8,128)S(1)} %constant_dynamic-update-slice_fusion.st0), channel_id=1, source_target_pairs={{0,1},{1,0},{2,3},{3,2},{4,5},{5,4},{6,7},{7,6},{8,9},{9,8},{10,11... | collective-permute-start | bytes 491528 | tf_op jit(solution)/shard_map/ppermute | solution.py:262
  17.5 11.6 %collective-permute-start.7 = (f32[8,8,1024]{2,1,0:T(8,128)S(1)}, f32[8,8,1024]{2,1,0:T(8,128)S(1)}, u32[]{:S(2)}, u32[]{:S(2)}) collective-permute-start(f32[8,8,1024]{2,1,0:T(8,128)S(1)} %pad_maximum_fusion), channel_id=1, source_target_pairs={{0,1},{1,0},{2,3},{3,2},{4,5},{5,4},{6,7},{7,6},{8,9},{9,8},{10,11... | collective-permute-start | bytes 786440 | tf_op jit(solution)/shard_map/ppermute | solution.py:262

commit v3 on v2

--- a/solution.py
+++ b/solution.py
@@ -11,6 +11,7 @@
 TS = 32
 LANES = 128
 STEP = 256
+WAYS = 16
 
 A0, A1, A2, A3 = 3.1415628696601985, -5.166617869525222, 2.538088675224665, -0.546492984410238
 B0, B1, B2 = A0 / A3, A1 / A3, A2 / A3
@@ -68,19 +69,22 @@
 
 
 def place(mask, size):
-    at, order, bit = 0 * mask, 0, size // 2
-    while bit:
-        at = at + ((mask // bit) % 2) * (1 << order)
-        order, bit = order + 1, bit // 2
+    bits = size.bit_length() - 1
+    at = 0 * mask
+    for order in range(bits):
+        at = at | (((mask >> (bits - 1 - order)) & 1) << order)
     return at
 
 
-def add_sources(chans, directions, depth, so_ref, lhs, total, both0, both1, sides0, sides1):
+def add_sources(chans, directions, depth, so_ref, lhs, total, *work):
+    both, sides = work[:2], work[2:]
     shards, _, width = so_ref.shape
     step = math.gcd(width, STEP)
     per = width // step
-    last = shards * per // 2
-    sides1[...] = jnp.zeros_like(sides1)
+    half = 2 * chans * TS
+    last = shards * per
+    ways = math.gcd(last, WAYS)
+    sides[-1][...] = jnp.zeros_like(sides[-1])
 
     def part(t):
         return so_ref[t // per, :, pl.ds(pl.multiple_of(lax.rem(t, per) * step, step), step)]
@@ -95,7 +99,7 @@
             for c in range(chans):
                 at = (side * chans + c) * TS
                 turns = both[at : at + TS]
-                size = both[2 * LANES + at : 2 * LANES + at + TS]
+                size = both[half + at : half + at + TS]
                 if side == 0:
                     size = size * weights[c : c + 1]
                 re, im = phasor(turns, size)
@@ -103,40 +107,40 @@
                 sides[2 * at + TS : 2 * at + 2 * TS] = im.astype(jnp.bfloat16)
 
     def collect(sides):
-        for at in range(0, 2 * chans * TS, LANES):
-            total[at : at + LANES] += lax.dot_general(
-                sides[at : at + LANES],
-                sides[2 * chans * TS + at : 2 * chans * TS + at + LANES],
-                (((1,), (1,)), ((), ())),
-                preferred_element_type=jnp.float32,
-            )
-
-    product(0, both0)
+        whole = lax.dot_general(
+            sides[:half], sides[half:], (((1,), (1,)), ((), ())), preferred_element_type=jnp.float32
+        )
+        for at in range(0, half, LANES):
+            total[at : at + LANES] += whole[at : at + LANES, at : at + LANES]
+
+    product(0, both[0])
 
     def turn(t, carry):
-        product(last + t, both1)
-        phasors(t, both0, sides0)
-        collect(sides1)
-        product(jnp.minimum(t + 1, last - 1), both0)
-        phasors(last + t, both1, sides1)
-        collect(sides0)
+        for way in range(ways):
+            at = t * ways + way
+            product(jnp.minimum(at + 1, last - 1), both[(way + 1) % 2])
+            phasors(at, both[way % 2], sides[way % 2])
+            collect(sides[(way + 1) % 2])
         return carry
 
-    lax.fori_loop(0, last, turn, 0)
-    collect(sides1)
+    lax.fori_loop(0, last // ways, turn, 0)
+    collect(sides[-1])
 
 
 def first_kernel(chans, directions, depth, row, size, pairs_ref, st0, st1, so_ref, lhs, total, *work):
-    held = st0.shape[0]
     total[...] = jnp.zeros_like(total)
+    if row is not None:
+        me = lax.axis_index("src")
+        pair = place(pairs_ref[pl.ds(me * row[0] + row[1], 1)] ^ me, size)
     for side in range(2):
         if row is None:
-            at = side
+            block = st0[side]
         else:
-            me = lax.axis_index("src")
-            at = place(pairs_ref[me * row[0] + row[1], side] ^ me, size)
-        low = lax.rem(at, held)
-        block = jnp.where(at < held, st0[low], st1[low])
+            at = jnp.broadcast_to(pair[:, side : side + 1], st0.shape[1:])
+            block = jnp.zeros(st0.shape[1:], jnp.float32)
+            for n in range(st0.shape[0]):
+                block = jnp.where(at == n, st0[n], block)
+                block = jnp.where(at == n + st0.shape[0], st1[n], block)
         phase, amplitude = station_rows(block, directions, depth)
         lhs[side * LANES : (side + 1) * LANES] = phase
         lhs[(2 + side) * LANES : (3 + side) * LANES] = amplitude
@@ -152,7 +156,8 @@
     total[...] = before[...]
     add_sources(chans, directions, depth, so_ref, lhs, total, *work)
     me = lax.axis_index("src") * row[0] + row[1]
-    same = pairs_ref[me, 0] == pairs_ref[me, 1]
+    pair = pairs_ref[pl.ds(me, 1)]
+    same = pair[:, 0:1] == pair[:, 1:2]
     high = lax.broadcasted_iota(jnp.int32, (8, LANES), 0)
     lane = lax.broadcasted_iota(jnp.int32, (8, LANES), 1)
     fold = LANES // TS
@@ -181,22 +186,18 @@
         self.chans, self.directions = chans, directions
         self.depth = -(-(SOURCE_ROWS + 3 * directions) // LANES) * LANES
         step = math.gcd(width, STEP)
-        self.work = [
-            pltpu.VMEM((4 * LANES, step), jnp.float32),
-            pltpu.VMEM((4 * LANES, step), jnp.float32),
-            pltpu.VMEM((4 * chans * TS, step), jnp.bfloat16),
-            pltpu.VMEM((4 * chans * TS, step), jnp.bfloat16),
-        ]
+        self.work = [pltpu.VMEM((4 * chans * TS, step), jnp.float32)] * 2
+        self.work += [pltpu.VMEM((4 * chans * TS, step), jnp.bfloat16)] * 2
         self.total = (2 * chans * TS, LANES)
 
-    def call(self, kernel, out_shape, in_specs, scratch, args):
+    def call(self, kernel, out_shape, scratch, args):
         vmem = pl.BlockSpec(memory_space=pltpu.VMEM)
         sources = args[-1].shape[0] * args[-1].shape[2]
         count = 2 * self.chans * TS * sources
         return pl.pallas_call(
             kernel,
             out_shape=out_shape,
-            in_specs=in_specs + [vmem] * (len(args) - len(in_specs)),
+            in_specs=[vmem] * len(args),
             out_specs=jax.tree.map(lambda _: vmem, out_shape),
             scratch_shapes=scratch,
             compiler_params=pltpu.CompilerParams(vmem_limit_bytes=32 << 20),
@@ -209,20 +210,18 @@
             jax.ShapeDtypeStruct((4 * LANES, self.depth), jnp.bfloat16),
             jax.ShapeDtypeStruct(self.total, jnp.float32),
         )
-        smem = pl.BlockSpec(memory_space=pltpu.SMEM)
-        return self.call(kernel, shapes, [smem], self.work, (pairs, *stations, sources))
+        return self.call(kernel, shapes, self.work, (pairs, *stations, sources))
 
     def next(self, lhs, total, sources):
         kernel = functools.partial(next_kernel, self.chans, self.directions, self.depth)
         shape = jax.ShapeDtypeStruct(self.total, jnp.float32)
-        return self.call(kernel, shape, [], self.work, (lhs, total, sources))
+        return self.call(kernel, shape, self.work, (lhs, total, sources))
 
     def last(self, row, pairs, lhs, total, sources):
         kernel = functools.partial(last_kernel, self.chans, self.directions, self.depth, row)
         shape = jax.ShapeDtypeStruct((self.chans, 2, TS * TS), jnp.float32)
-        smem = pl.BlockSpec(memory_space=pltpu.SMEM)
         scratch = [pltpu.VMEM(self.total, jnp.float32)] + self.work
-        return self.call(kernel, shape, [smem], scratch, (pairs, lhs, total, sources))
+        return self.call(kernel, shape, scratch, (pairs, lhs, total, sources))
 
 
 def pack_kernel(scale, chans, channel_ref, positions_ref, flux_ref, cluster_ref, jones_ref, uvw_ref, station_ref, source_ref):
@@ -262,14 +261,22 @@
     return lax.ppermute(x, "src", [(i, i ^ bit) for i in range(size)])
 
 
-def spread(station, size):
+def after(x, *earlier):
+    return lax.optimization_barrier((x, *earlier))[0]
+
+
+def spread(station, source, size):
     bit = size // 2
+    got = None
     while bit:
-        got = swap(station, bit, size)
+        arrived = swap(station, bit, size)
         if bit > 1:
-            station = jnp.concatenate([station, got], 0)
+            got = swap(source if got is None else after(source, arrived), bit, size)
+            station = jnp.concatenate([station, arrived], 0)
+        if bit > 2:
+            source = jnp.concatenate([source, got], 0)
         bit //= 2
-    return station, got
+    return (station, arrived), source, got
 
 
 def on_device(positions, flux, cluster, jones, station_uvw, channels, tile_map):
@@ -277,11 +284,7 @@
     chans, _, directions, own = jones.shape
     scale = 1.0 / math.sqrt(positions.shape[1] * size)
     station, source = pack(positions, flux, cluster, jones, station_uvw, channels, scale)
-    stations = spread(station, size)
-    bit = size // 2
-    while bit > 2:
-        source = jnp.concatenate([source, swap(source, bit, size)], 0)
-        bit //= 2
+    stations, source, got = spread(station, source, size)
     own_rows = tile_map.shape[0] // size
     many = TS // own
     predictor = Predictor(chans, directions, positions.shape[1])
@@ -298,8 +301,7 @@
             picked = picked.reshape(2, many, whole.shape[1], chans, own)
             picked = jnp.transpose(picked, (0, 2, 3, 1, 4)).reshape(2, whole.shape[1], chans * TS)
             begun.append(predictor.first(None, size, tile_map, (picked, picked), source))
-    got = swap(source, 2, size)
-    both = jnp.concatenate([source, got], 0)
+    both = jnp.concatenate([after(source, begun[-1][-1]), got], 0)
     other = swap(both, 1, size)
     out = []
     for row, (lhs, total) in enumerate(begun):

time: 38.7 us -> 33.9 us (0.88)
  Pallas kernels: 19.8 us -> 15.8 us
  starting transfers between devices: 15.4 us -> 13.8 us
  local copies, waits for them, and re-layouts: 0.91 us -> 1.58 us
    pallas_call x3, Pallas kernels: 18.3 us -> 14.3 us  [call(): pl.pallas_call(kernel, out_shape=out_shape, in_specs=[vmem] * len(args),...]
    ppermute x8, starting transfers between devices: 15.4 us -> 13.8 us  [swap(): return lax.ppermute(x, 'src', [(i, i ^ bit) for i in range(size)])]
    unnamed x12, local copies, waits for them, and re-layouts: 0.9 us -> 1.57 us
  transfers between devices with their start and end apart: 8 -> 8, of which waited for: 3 -> 3; matrix products, arithmetic and copies ran while one was open for 2% -> 3% of each run, Pallas kernels for 23% -> 21%
where the time goes in v3:
time: 33.9 us; the launch traced here: 33.7 us
  Pallas kernels  15.8 us (47%)
  starting transfers between devices  13.8 us (41%)
  waiting for transfers between devices  2.3 us (7%)
  local copies, waits for them, and re-layouts  1.58 us (5%)
    pallas_call x3, Pallas kernels, call(): pl.pallas_call(kernel, out_shape=out_shape, in_specs=[vmem] * len(args),...  14.3 us
    ppermute x8, starting transfers between devices, swap(): return lax.ppermute(x, 'src', [(i, i ^ bit) for i in range(size)])  13.8 us
    ppermute x8, waiting for transfers between devices, swap(): return lax.ppermute(x, 'src', [(i, i ^ bit) for i in range(size)])  2.3 us
    unnamed x12, local copies, waits for them, and re-layouts  1.57 us
    pallas_call x1, Pallas kernels, pack(): pl.pallas_call(functools.partial(pack_kernel, scale, chans), out_shape=(j...  1.55 us
  transfers between devices with their start and end apart: 8, of which 3 were waited for; matrix products, arithmetic and copies ran while one was open for 3% of the time, Pallas kernels for 21%

profile of v3, /device:TPU:1, one launch (start us, length us, event | category | flops | bytes accessed | tf_op | source)
XLA Modules:
  0.0 33.7 jit_solution(8210302566792890947)
XLA Ops:
  0.0 1.5 %shard_map.73 = (f32[1,40,128]{2,1,0:T(8,128)}, f32[1,8,1024]{2,1,0:T(8,128)}) custom-call(s32[4]{0:T(128)} %channel_ref.1, f32[2,1024]{1,0:T(2,128)} %positions_ref.1, f32[4,1024]{1,0:T(4,128)} %flux_ref.1, s32[1,1024]{1,0:T(1,128)} %bitcast.2, f32[4,2,16,32]{3,2,1,0:T(8,128)} %jones_ref.1, f32[3,32]{1,0:T(4,128)} %uvw_ref.1), custom_call_target="tpu_custom_call" | custom-call | tf_op jit(solution)/shard_map/pallas_call | solution.py:249
  1.5 3.1 %collective-permute-start = (f32[1,40,128]{2,1,0:T(8,128)}, f32[1,40,128]{2,1,0:T(8,128)S(1)}, u32[]{:S(2)}, u32[]{:S(2)}) collective-permute-start(f32[1,40,128]{2,1,0:T(8,128)} %get-tuple-element.12), channel_id=1, source_target_pairs={{0,8},{1,9},{2,10},{3,11},{4,12},{5,13},{6,14},{7,15},{8,0},{9,1},... | collective-permute-start | bytes 61448 | tf_op jit(solution)/shard_map/ppermute | solution.py:261
  4.7 0.1 collective-permute-start.4
  4.8 0.8 %constant_dynamic-update-slice_fusion.6 = f32[4,8,1024]{2,1,0:T(8,128)S(1)} fusion(f32[1,8,1024]{2,1,0:T(8,128)} %get-tuple-element.13), kind=kLoop, calls=%fused_computation.10 | loop fusion | bytes 65536
  5.6 0.0 copy-done
  5.6 0.7 %copy-done.2 = s32[16,2]{0,1:T(2,128)S(1)} copy-done((s32[16,2]{0,1:T(2,128)S(1)}, s32[16,2]{0,1:T(2,128)}, u32[]{:S(2)}) %copy-start.2) | copy-done | bytes 152
  6.2 0.1 copy.9.pairs_ref
  6.3 0.0 collective-permute-done
  6.3 1.4 %collective-permute-start.1 = (f32[2,40,128]{2,1,0:T(8,128)S(1)}, f32[2,40,128]{2,1,0:T(8,128)S(1)}, u32[]{:S(2)}, u32[]{:S(2)}) collective-permute-start(f32[2,40,128]{2,1,0:T(8,128)S(1)} %pad_maximum_fusion.3), channel_id=1, source_target_pairs={{0,4},{1,5},{2,6},{3,7},{4,0},{5,1},{6,2},{7,3},{8,12},{9,13},{10,... | collective-permute-start | bytes 122888 | tf_op jit(solution)/shard_map/ppermute | solution.py:261
  7.7 0.9 %collective-permute-done.4 = f32[1,8,1024]{2,1,0:T(8,128)S(1)} collective-permute-done((f32[1,8,1024]{2,1,0:T(8,128)}, f32[1,8,1024]{2,1,0:T(8,128)S(1)}, u32[]{:S(2)}, u32[]{:S(2)}) %collective-permute-start.4) | collective-permute-done | bytes 32800 | tf_op jit(solution)/shard_map/ppermute | solution.py:261
  8.6 0.6 %collective-permute-done.1 = f32[2,40,128]{2,1,0:T(8,128)S(1)} collective-permute-done((f32[2,40,128]{2,1,0:T(8,128)S(1)}, f32[2,40,128]{2,1,0:T(8,128)S(1)}, u32[]{:S(2)}, u32[]{:S(2)}) %collective-permute-start.1) | collective-permute-done | bytes 40992 | tf_op jit(solution)/shard_map/ppermute | solution.py:261
  9.3 1.2 %collective-permute-start.2 = (f32[4,40,128]{2,1,0:T(8,128)S(1)}, f32[4,40,128]{2,1,0:T(8,128)S(1)}, u32[]{:S(2)}, u32[]{:S(2)}) collective-permute-start(f32[4,40,128]{2,1,0:T(8,128)S(1)} %pad_maximum_fusion.1), channel_id=1, source_target_pairs={{0,2},{1,3},{2,0},{3,1},{4,6},{5,7},{6,4},{7,5},{8,10},{9,11},{10,... | collective-permute-start | bytes 245768 | tf_op jit(solution)/shard_map/ppermute | solution.py:261
  10.5 1.3 %collective-permute-start.5 = (f32[2,8,1024]{2,1,0:T(8,128)S(1)}, f32[2,8,1024]{2,1,0:T(8,128)S(1)}, u32[]{:S(2)}, u32[]{:S(2)}) collective-permute-start(f32[2,8,1024]{2,1,0:T(8,128)S(1)} %pad_maximum_fusion.2), channel_id=1, source_target_pairs={{0,4},{1,5},{2,6},{3,7},{4,0},{5,1},{6,2},{7,3},{8,12},{9,13},{10,... | collective-permute-start | bytes 196616 | tf_op jit(solution)/shard_map/ppermute | solution.py:261
  11.8 0.8 %collective-permute-done.2 = f32[4,40,128]{2,1,0:T(8,128)S(1)} collective-permute-done((f32[4,40,128]{2,1,0:T(8,128)S(1)}, f32[4,40,128]{2,1,0:T(8,128)S(1)}, u32[]{:S(2)}, u32[]{:S(2)}) %collective-permute-start.2) | collective-permute-done | bytes 81952 | tf_op jit(solution)/shard_map/ppermute | solution.py:261
  12.6 3.6 %collective-permute-start.3 = (f32[8,40,128]{2,1,0:T(8,128)S(1)}, f32[8,40,128]{2,1,0:T(8,128)S(1)}, u32[]{:S(2)}, u32[]{:S(2)}) collective-permute-start(f32[8,40,128]{2,1,0:T(8,128)S(1)} %constant_dynamic-update-slice_fusion.st0), channel_id=1, source_target_pairs={{0,1},{1,0},{2,3},{3,2},{4,5},{5,4},{6,7},{7,6},{8,9},{9,8},{10,11... | collective-permute-start | bytes 491528 | tf_op jit(solution)/shard_map/ppermute | solution.py:261
  16.2 0.0 collective-permute-done.5
  16.2 1.7 %collective-permute-start.6 = (f32[4,8,1024]{2,1,0:T(8,128)S(1)}, f32[4,8,1024]{2,1,0:T(8,128)S(1)}, u32[]{:S(2)}, u32[]{:S(2)}) collective-permute-start(f32[4,8,1024]{2,1,0:T(8,128)S(1)} %constant_dynamic-update-slice_fusion.4.so_ref), channel_id=1, source_target_pairs={{0,2},{1,3},{2,0},{3,1},{4,6},{5,7},{6,4},{7,5},{8,10},{9,11},{10,... | collective-permute-start | bytes 393224 | tf_op jit(solution)/shard_map/ppermute | solution.py:261
  17.9 0.0 collective-permute-done.3.st1
  17.9 3.6 %shard_map.74 = (bf16[512,128]{1,0:T(8,128)(2,1)S(1)}, f32[256,128]{1,0:T(8,128)S(1)}) custom-call(s32[16,2]{1,0:T(8,128)S(1)} %copy.9.pairs_ref, f32[8,40,128]{2,1,0:T(8,128)S(1)} %constant_dynamic-update-slice_fusion.st0, f32[8,40,128]{2,1,0:T(8,128)S(1)} %collective-permute-done.3.st1, f32[4,8,1024]{2,1,0:T(8,128)S(1)} %constant_dynamic-update-slice_fusion.4.so_ref), custom_call_target="tpu_custom_call" | custom-call | flops 2097152000 | tf_op jit(solution)/shard_map/pallas_call | solution.py:197
  21.5 0.0 collective-permute-done.6.so_ref
  21.5 1.4 %collective-permute-start.7 = (f32[8,8,1024]{2,1,0:T(8,128)S(1)}, f32[8,8,1024]{2,1,0:T(8,128)S(1)}, u32[]{:S(2)}, u32[]{:S(2)}) collective-permute-start(f32[8,8,1024]{2,1,0:T(8,128)S(1)} %pad_maximum_fusion), channel_id=1, source_target_pairs={{0,1},{1,0},{2,3},{3,2},{4,5},{5,4},{6,7},{7,6},{8,9},{9,8},{10,11... | collective-permute-start | bytes 786440 | tf_op jit(solution)/shard_map/ppermute | solution.py:261
  22.9 3.4 %shard_map.75.before = f32[256,128]{1,0:T(8,128)S(1)} custom-call(bf16[512,128]{1,0:T(8,128)(2,1)S(1)} %get-tuple-element.15.lhs, f32[256,128]{1,0:T(8,128)S(1)} %get-tuple-element.16.before, f32[4,8,1024]{2,1,0:T(8,128)S(1)} %collective-permute-done.6.so_ref), custom_call_target="tpu_custom_call" | custom-call | flops 2097152000 | tf_op jit(solution)/shard_map/pallas_call | solution.py:197
  26.3 0.0 collective-permute-done.7.so_ref
  26.3 7.3 %shard_map.76 = f32[4,2,1024]{2,1,0:T(2,128)} custom-call(s32[16,2]{1,0:T(8,128)S(1)} %copy.9.pairs_ref, bf16[512,128]{1,0:T(8,128)(2,1)S(1)} %get-tuple-element.15.lhs, f32[256,128]{1,0:T(8,128)S(1)} %shard_map.75.before, f32[8,8,1024]{2,1,0:T(8,128)S(1)} %collective-permute-done.7.so_ref), custom_call_target="tpu_custom_call" | custom-call | flops 4194304000 | tf_op jit(solution)/shard_map/pallas_call | solution.py:197
  (14 shorter events, 0.1 us)
Async XLA Ops:
  1.5 4.8 %collective-permute-start = (f32[1,40,128]{2,1,0:T(8,128)}, f32[1,40,128]{2,1,0:T(8,128)S(1)}, u32[]{:S(2)}, u32[]{:S(2)}) collective-permute-start(f32[1,40,128]{2,1,0:T(8,128)} %get-tuple-element.12), channel_id=1, source_target_pairs={{0,8},{1,9},{2,10},{3,11},{4,12},{5,13},{6,14},{7,15},{8,0},{9,1},... | collective-permute-start | bytes 61448 | tf_op jit(solution)/shard_map/ppermute | solution.py:261
  4.7 0.9 %copy-start = (f32[1,40,128]{2,1,0:T(8,128)S(1)}, f32[1,40,128]{2,1,0:T(8,128)}, u32[]{:S(2)}) copy-start(f32[1,40,128]{2,1,0:T(8,128)} %get-tuple-element.12) | copy-start | bytes 61444
  4.7 3.9 %collective-permute-start.4 = (f32[1,8,1024]{2,1,0:T(8,128)}, f32[1,8,1024]{2,1,0:T(8,128)S(1)}, u32[]{:S(2)}, u32[]{:S(2)}) collective-permute-start(f32[1,8,1024]{2,1,0:T(8,128)} %get-tuple-element.13), channel_id=1, source_target_pairs={{0,8},{1,9},{2,10},{3,11},{4,12},{5,13},{6,14},{7,15},{8,0},{9,1},... | collective-permute-start | bytes 98312 | tf_op jit(solution)/shard_map/ppermute | solution.py:261
  5.6 0.7 %copy-start.2 = (s32[16,2]{0,1:T(2,128)S(1)}, s32[16,2]{0,1:T(2,128)}, u32[]{:S(2)}) copy-start(s32[16,2]{0,1:T(2,128)} %param.13) | copy-start | bytes 388
  6.3 2.3 %copy-start.1 = (f32[1,8,1024]{2,1,0:T(8,128)S(1)}, f32[1,8,1024]{2,1,0:T(8,128)}, u32[]{:S(2)}) copy-start(f32[1,8,1024]{2,1,0:T(8,128)} %get-tuple-element.13) | copy-start | bytes 98308
  6.3 2.9 %collective-permute-start.1 = (f32[2,40,128]{2,1,0:T(8,128)S(1)}, f32[2,40,128]{2,1,0:T(8,128)S(1)}, u32[]{:S(2)}, u32[]{:S(2)}) collective-permute-start(f32[2,40,128]{2,1,0:T(8,128)S(1)} %pad_maximum_fusion.3), channel_id=1, source_target_pairs={{0,4},{1,5},{2,6},{3,7},{4,0},{5,1},{6,2},{7,3},{8,12},{9,13},{10,... | collective-permute-start | bytes 122888 | tf_op jit(solution)/shard_map/ppermute | solution.py:261
  9.3 3.3 %collective-permute-start.2 = (f32[4,40,128]{2,1,0:T(8,128)S(1)}, f32[4,40,128]{2,1,0:T(8,128)S(1)}, u32[]{:S(2)}, u32[]{:S(2)}) collective-permute-start(f32[4,40,128]{2,1,0:T(8,128)S(1)} %pad_maximum_fusion.1), channel_id=1, source_target_pairs={{0,2},{1,3},{2,0},{3,1},{4,6},{5,7},{6,4},{7,5},{8,10},{9,11},{10,... | collective-permute-start | bytes 245768 | tf_op jit(solution)/shard_map/ppermute | solution.py:261
  10.5 5.7 %collective-permute-start.5 = (f32[2,8,1024]{2,1,0:T(8,128)S(1)}, f32[2,8,1024]{2,1,0:T(8,128)S(1)}, u32[]{:S(2)}, u32[]{:S(2)}) collective-permute-start(f32[2,8,1024]{2,1,0:T(8,128)S(1)} %pad_maximum_fusion.2), channel_id=1, source_target_pairs={{0,4},{1,5},{2,6},{3,7},{4,0},{5,1},{6,2},{7,3},{8,12},{9,13},{10,... | collective-permute-start | bytes 196616 | tf_op jit(solution)/shard_map/ppermute | solution.py:261
  12.6 5.3 %collective-permute-start.3 = (f32[8,40,128]{2,1,0:T(8,128)S(1)}, f32[8,40,128]{2,1,0:T(8,128)S(1)}, u32[]{:S(2)}, u32[]{:S(2)}) collective-permute-start(f32[8,40,128]{2,1,0:T(8,128)S(1)} %constant_dynamic-update-slice_fusion.st0), channel_id=1, source_target_pairs={{0,1},{1,0},{2,3},{3,2},{4,5},{5,4},{6,7},{7,6},{8,9},{9,8},{10,11... | collective-permute-start | bytes 491528 | tf_op jit(solution)/shard_map/ppermute | solution.py:261
  16.2 5.3 %collective-permute-start.6 = (f32[4,8,1024]{2,1,0:T(8,128)S(1)}, f32[4,8,1024]{2,1,0:T(8,128)S(1)}, u32[]{:S(2)}, u32[]{:S(2)}) collective-permute-start(f32[4,8,1024]{2,1,0:T(8,128)S(1)} %constant_dynamic-update-slice_fusion.4.so_ref), channel_id=1, source_target_pairs={{0,2},{1,3},{2,0},{3,1},{4,6},{5,7},{6,4},{7,5},{8,10},{9,11},{10,... | collective-permute-start | bytes 393224 | tf_op jit(solution)/shard_map/ppermute | solution.py:261
  21.5 4.8 %collective-permute-start.7 = (f32[8,8,1024]{2,1,0:T(8,128)S(1)}, f32[8,8,1024]{2,1,0:T(8,128)S(1)}, u32[]{:S(2)}, u32[]{:S(2)}) collective-permute-start(f32[8,8,1024]{2,1,0:T(8,128)S(1)} %pad_maximum_fusion), channel_id=1, source_target_pairs={{0,1},{1,0},{2,3},{3,2},{4,5},{5,4},{6,7},{7,6},{8,9},{9,8},{10,11... | collective-permute-start | bytes 786440 | tf_op jit(solution)/shard_map/ppermute | solution.py:261

commit v4 on v3

--- a/solution.py
+++ b/solution.py
@@ -45,7 +45,8 @@
     none = jnp.zeros((SOURCE_ROWS, block.shape[1]), jnp.float32)
     phase = jnp.concatenate([u0, u0, u1, u0, u2, u1, t0, t1, t2, pad], 0)
     amplitude = jnp.concatenate([none, g0, g1, g2, pad], 0)
-    return phase.T.astype(jnp.bfloat16), amplitude.T.astype(jnp.bfloat16)
+    rest = jnp.zeros((LANES - directions, block.shape[1]), jnp.float32)
+    return phase.T.astype(jnp.bfloat16), amplitude.T.astype(jnp.bfloat16), jnp.concatenate([size, rest], 0).T
 
 
 def source_rows(src, directions, depth):
@@ -68,15 +69,23 @@
     return size * (0.5 * TOP - q), (size * s) * c
 
 
+def steps(size):
+    high = [1 << n for n in range(size.bit_length() - 2, 1, -1)]
+    return high[:1] + [2] + high[1:] + [1]
+
+
 def place(mask, size):
-    bits = size.bit_length() - 1
     at = 0 * mask
-    for order in range(bits):
-        at = at | (((mask >> (bits - 1 - order)) & 1) << order)
+    for order, bit in enumerate(steps(size)):
+        at = at | (((mask >> (bit.bit_length() - 1)) & 1) << order)
     return at
 
 
-def add_sources(chans, directions, depth, so_ref, lhs, total, *work):
+def look_up(table, lanes):
+    return jnp.take_along_axis(table, lanes, axis=1, mode="promise_in_bounds")
+
+
+def add_sources(chans, directions, depth, so_ref, lhs, sizes, total, *work):
     both, sides = work[:2], work[2:]
     shards, _, width = so_ref.shape
     step = math.gcd(width, STEP)
@@ -94,14 +103,17 @@
         into[...] = jnp.dot(lhs[...], made, preferred_element_type=jnp.float32)
 
     def phasors(t, both, sides):
-        weights = part(t)[4:]
+        src = part(t)
+        kinds = jnp.broadcast_to(src[3:4].astype(jnp.int32), (TS, step))
         for side in range(2):
             for c in range(chans):
                 at = (side * chans + c) * TS
                 turns = both[at : at + TS]
-                size = both[half + at : half + at + TS]
                 if side == 0:
-                    size = size * weights[c : c + 1]
+                    size = both[half + at : half + at + TS] * src[4 + c : 5 + c]
+                else:
+                    table = sizes[c * TS : (c + 1) * TS]
+                    size = jnp.concatenate([look_up(table, kinds[:, n : n + LANES]) for n in range(0, step, LANES)], 1)
                 re, im = phasor(turns, size)
                 sides[2 * at : 2 * at + TS] = re.astype(jnp.bfloat16)
                 sides[2 * at + TS : 2 * at + 2 * TS] = im.astype(jnp.bfloat16)
@@ -127,7 +139,7 @@
     collect(sides[-1])
 
 
-def first_kernel(chans, directions, depth, row, size, pairs_ref, st0, st1, so_ref, lhs, total, *work):
+def first_kernel(chans, directions, depth, row, size, pairs_ref, st0, st1, so_ref, lhs, sizes, total, *work):
     total[...] = jnp.zeros_like(total)
     if row is not None:
         me = lax.axis_index("src")
@@ -141,20 +153,23 @@
             for n in range(st0.shape[0]):
                 block = jnp.where(at == n, st0[n], block)
                 block = jnp.where(at == n + st0.shape[0], st1[n], block)
-        phase, amplitude = station_rows(block, directions, depth)
+        phase, amplitude, size = station_rows(block, directions, depth)
         lhs[side * LANES : (side + 1) * LANES] = phase
-        lhs[(2 + side) * LANES : (3 + side) * LANES] = amplitude
-    add_sources(chans, directions, depth, so_ref, lhs, total, *work)
-
-
-def next_kernel(chans, directions, depth, lhs, before, so_ref, total, *work):
+        if side == 0:
+            lhs[2 * LANES : 3 * LANES] = amplitude
+        else:
+            sizes[...] = size
+    add_sources(chans, directions, depth, so_ref, lhs, sizes, total, *work)
+
+
+def next_kernel(chans, directions, depth, lhs, sizes, before, so_ref, total, *work):
     total[...] = before[...]
-    add_sources(chans, directions, depth, so_ref, lhs, total, *work)
-
-
-def last_kernel(chans, directions, depth, row, pairs_ref, lhs, before, so_ref, out_ref, total, *work):
+    add_sources(chans, directions, depth, so_ref, lhs, sizes, total, *work)
+
+
+def last_kernel(chans, directions, depth, row, pairs_ref, lhs, sizes, before, so_ref, out_ref, total, *work):
     total[...] = before[...]
-    add_sources(chans, directions, depth, so_ref, lhs, total, *work)
+    add_sources(chans, directions, depth, so_ref, lhs, sizes, total, *work)
     me = lax.axis_index("src") * row[0] + row[1]
     pair = pairs_ref[pl.ds(me, 1)]
     same = pair[:, 0:1] == pair[:, 1:2]
@@ -186,7 +201,7 @@
         self.chans, self.directions = chans, directions
         self.depth = -(-(SOURCE_ROWS + 3 * directions) // LANES) * LANES
         step = math.gcd(width, STEP)
-        self.work = [pltpu.VMEM((4 * chans * TS, step), jnp.float32)] * 2
+        self.work = [pltpu.VMEM((3 * chans * TS, step), jnp.float32)] * 2
         self.work += [pltpu.VMEM((4 * chans * TS, step), jnp.bfloat16)] * 2
         self.total = (2 * chans * TS, LANES)
 
@@ -207,21 +222,22 @@
     def first(self, row, size, pairs, stations, sources):
         kernel = functools.partial(first_kernel, self.chans, self.directions, self.depth, row, size)
         shapes = (
-            jax.ShapeDtypeStruct((4 * LANES, self.depth), jnp.bfloat16),
+            jax.ShapeDtypeStruct((3 * LANES, self.depth), jnp.bfloat16),
+            jax.ShapeDtypeStruct((LANES, LANES), jnp.float32),
             jax.ShapeDtypeStruct(self.total, jnp.float32),
         )
         return self.call(kernel, shapes, self.work, (pairs, *stations, sources))
 
-    def next(self, lhs, total, sources):
+    def next(self, lhs, sizes, total, sources):
         kernel = functools.partial(next_kernel, self.chans, self.directions, self.depth)
         shape = jax.ShapeDtypeStruct(self.total, jnp.float32)
-        return self.call(kernel, shape, self.work, (lhs, total, sources))
-
-    def last(self, row, pairs, lhs, total, sources):
+        return self.call(kernel, shape, self.work, (lhs, sizes, total, sources))
+
+    def last(self, row, pairs, lhs, sizes, total, sources):
         kernel = functools.partial(last_kernel, self.chans, self.directions, self.depth, row)
         shape = jax.ShapeDtypeStruct((self.chans, 2, TS * TS), jnp.float32)
         scratch = [pltpu.VMEM(self.total, jnp.float32)] + self.work
-        return self.call(kernel, shape, scratch, (pairs, lhs, total, sources))
+        return self.call(kernel, shape, scratch, (pairs, lhs, sizes, total, sources))
 
 
 def pack_kernel(scale, chans, channel_ref, positions_ref, flux_ref, cluster_ref, jones_ref, uvw_ref, station_ref, source_ref):
@@ -266,17 +282,15 @@
 
 
 def spread(station, source, size):
-    bit = size // 2
-    got = None
-    while bit:
+    arrived = None
+    for bit in steps(size):
+        ready = source if arrived is None else after(source, arrived)
         arrived = swap(station, bit, size)
+        if bit > 2:
+            source = jnp.concatenate([source, swap(ready, bit, size)], 0)
         if bit > 1:
-            got = swap(source if got is None else after(source, arrived), bit, size)
             station = jnp.concatenate([station, arrived], 0)
-        if bit > 2:
-            source = jnp.concatenate([source, got], 0)
-        bit //= 2
-    return (station, arrived), source, got
+    return (station, arrived), source, swap(after(source, station), 2, size)
 
 
 def on_device(positions, flux, cluster, jones, station_uvw, channels, tile_map):
@@ -304,9 +318,9 @@
     both = jnp.concatenate([after(source, begun[-1][-1]), got], 0)
     other = swap(both, 1, size)
     out = []
-    for row, (lhs, total) in enumerate(begun):
-        total = predictor.next(lhs, total, got)
-        out.append(predictor.last((own_rows, row), tile_map, lhs, total, other))
+    for row, (lhs, sizes, total) in enumerate(begun):
+        total = predictor.next(lhs, sizes, total, got)
+        out.append(predictor.last((own_rows, row), tile_map, lhs, sizes, total, other))
     return jnp.stack(out)
 
 

time: 33.9 us -> 33.6 us (level)
  waiting for transfers between devices: 2.3 us -> 3.43 us
  starting transfers between devices: 13.8 us -> 12.8 us
    ppermute x8, waiting for transfers between devices: 2.3 us -> 3.43 us  [swap(): return lax.ppermute(x, 'src', [(i, i ^ bit) for i in range(size)])]
    ppermute x8, starting transfers between devices: 13.8 us -> 12.8 us  [swap(): return lax.ppermute(x, 'src', [(i, i ^ bit) for i in range(size)])]
    pallas_call x3, Pallas kernels: 14.3 us -> 13.9 us  [call(): pl.pallas_call(kernel, out_shape=out_shape, in_specs=[vmem] * len(args),...]
where the time goes in v4:
time: 33.6 us; the launch traced here: 33.4 us
  Pallas kernels  15.5 us (46%)
  starting transfers between devices  12.8 us (38%)
  waiting for transfers between devices  3.43 us (10%)
  local copies, waits for them, and re-layouts  1.58 us (5%)
    pallas_call x3, Pallas kernels, call(): pl.pallas_call(kernel, out_shape=out_shape, in_specs=[vmem] * len(args),...  13.9 us
    ppermute x8, starting transfers between devices, swap(): return lax.ppermute(x, 'src', [(i, i ^ bit) for i in range(size)])  12.8 us
    ppermute x8, waiting for transfers between devices, swap(): return lax.ppermute(x, 'src', [(i, i ^ bit) for i in range(size)])  3.43 us
    unnamed x12, local copies, waits for them, and re-layouts  1.57 us
    pallas_call x1, Pallas kernels, pack(): pl.pallas_call(functools.partial(pack_kernel, scale, chans), out_shape=(j...  1.55 us
  transfers between devices with their start and end apart: 8, of which 3 were waited for; matrix products, arithmetic and copies ran while one was open for 3% of the time, Pallas kernels for 21%

profile of v4, /device:TPU:1, one launch (start us, length us, event | category | flops | bytes accessed | tf_op | source)
XLA Modules:
  0.0 33.4 jit_solution(17506303937773164452)
XLA Ops:
  0.0 1.5 %shard_map.73 = (f32[1,40,128]{2,1,0:T(8,128)}, f32[1,8,1024]{2,1,0:T(8,128)}) custom-call(s32[4]{0:T(128)} %channel_ref.1, f32[2,1024]{1,0:T(2,128)} %positions_ref.1, f32[4,1024]{1,0:T(4,128)} %flux_ref.1, s32[1,1024]{1,0:T(1,128)} %bitcast.2, f32[4,2,16,32]{3,2,1,0:T(8,128)} %jones_ref.1, f32[3,32]{1,0:T(4,128)} %uvw_ref.1), custom_call_target="tpu_custom_call" | custom-call | tf_op jit(solution)/shard_map/pallas_call | solution.py:265
  1.5 3.1 %collective-permute-start = (f32[1,40,128]{2,1,0:T(8,128)}, f32[1,40,128]{2,1,0:T(8,128)S(1)}, u32[]{:S(2)}, u32[]{:S(2)}) collective-permute-start(f32[1,40,128]{2,1,0:T(8,128)} %get-tuple-element.13), channel_id=1, source_target_pairs={{0,8},{1,9},{2,10},{3,11},{4,12},{5,13},{6,14},{7,15},{8,0},{9,1},... | collective-permute-start | bytes 61448 | tf_op jit(solution)/shard_map/ppermute | solution.py:277
  4.7 0.1 collective-permute-start.4
  4.8 0.8 %constant_dynamic-update-slice_fusion.6 = f32[4,8,1024]{2,1,0:T(8,128)S(1)} fusion(f32[1,8,1024]{2,1,0:T(8,128)} %get-tuple-element.14), kind=kLoop, calls=%fused_computation.10 | loop fusion | bytes 65536
  5.6 0.0 copy-done
  5.6 0.7 %copy-done.2 = s32[16,2]{0,1:T(2,128)S(1)} copy-done((s32[16,2]{0,1:T(2,128)S(1)}, s32[16,2]{0,1:T(2,128)}, u32[]{:S(2)}) %copy-start.2) | copy-done | bytes 152
  6.2 0.1 copy.9.pairs_ref
  6.3 0.0 collective-permute-done
  6.3 1.3 %collective-permute-start.1 = (f32[2,40,128]{2,1,0:T(8,128)S(1)}, f32[2,40,128]{2,1,0:T(8,128)S(1)}, u32[]{:S(2)}, u32[]{:S(2)}) collective-permute-start(f32[2,40,128]{2,1,0:T(8,128)S(1)} %pad_maximum_fusion.3), channel_id=1, source_target_pairs={{0,2},{1,3},{2,0},{3,1},{4,6},{5,7},{6,4},{7,5},{8,10},{9,11},{10,... | collective-permute-start | bytes 122888 | tf_op jit(solution)/shard_map/ppermute | solution.py:277
  7.6 1.0 %collective-permute-done.4 = f32[1,8,1024]{2,1,0:T(8,128)S(1)} collective-permute-done((f32[1,8,1024]{2,1,0:T(8,128)}, f32[1,8,1024]{2,1,0:T(8,128)S(1)}, u32[]{:S(2)}, u32[]{:S(2)}) %collective-permute-start.4) | collective-permute-done | bytes 32800 | tf_op jit(solution)/shard_map/ppermute | solution.py:277
  8.6 0.6 %collective-permute-done.1 = f32[2,40,128]{2,1,0:T(8,128)S(1)} collective-permute-done((f32[2,40,128]{2,1,0:T(8,128)S(1)}, f32[2,40,128]{2,1,0:T(8,128)S(1)}, u32[]{:S(2)}, u32[]{:S(2)}) %collective-permute-start.1) | collective-permute-done | bytes 40992 | tf_op jit(solution)/shard_map/ppermute | solution.py:277
  9.3 1.3 %collective-permute-start.2 = (f32[4,40,128]{2,1,0:T(8,128)S(1)}, f32[4,40,128]{2,1,0:T(8,128)S(1)}, u32[]{:S(2)}, u32[]{:S(2)}) collective-permute-start(f32[4,40,128]{2,1,0:T(8,128)S(1)} %pad_maximum_fusion.1), channel_id=1, source_target_pairs={{0,4},{1,5},{2,6},{3,7},{4,0},{5,1},{6,2},{7,3},{8,12},{9,13},{10,... | collective-permute-start | bytes 245768 | tf_op jit(solution)/shard_map/ppermute | solution.py:277
  10.6 0.2 collective-permute-start.5
  10.7 1.8 %collective-permute-done.2 = f32[4,40,128]{2,1,0:T(8,128)S(1)} collective-permute-done((f32[4,40,128]{2,1,0:T(8,128)S(1)}, f32[4,40,128]{2,1,0:T(8,128)S(1)}, u32[]{:S(2)}, u32[]{:S(2)}) %collective-permute-start.2) | collective-permute-done | bytes 81952 | tf_op jit(solution)/shard_map/ppermute | solution.py:277
  12.6 3.6 %collective-permute-start.3 = (f32[8,40,128]{2,1,0:T(8,128)S(1)}, f32[8,40,128]{2,1,0:T(8,128)S(1)}, u32[]{:S(2)}, u32[]{:S(2)}) collective-permute-start(f32[8,40,128]{2,1,0:T(8,128)S(1)} %constant_dynamic-update-slice_fusion.st0), channel_id=1, source_target_pairs={{0,1},{1,0},{2,3},{3,2},{4,5},{5,4},{6,7},{7,6},{8,9},{9,8},{10,11... | collective-permute-start | bytes 491528 | tf_op jit(solution)/shard_map/ppermute | solution.py:277
  16.2 0.0 collective-permute-done.5
  16.2 1.7 %collective-permute-start.6 = (f32[4,8,1024]{2,1,0:T(8,128)S(1)}, f32[4,8,1024]{2,1,0:T(8,128)S(1)}, u32[]{:S(2)}, u32[]{:S(2)}) collective-permute-start(f32[4,8,1024]{2,1,0:T(8,128)S(1)} %constant_dynamic-update-slice_fusion.4.so_ref), channel_id=1, source_target_pairs={{0,2},{1,3},{2,0},{3,1},{4,6},{5,7},{6,4},{7,5},{8,10},{9,11},{10,... | collective-permute-start | bytes 393224 | tf_op jit(solution)/shard_map/ppermute | solution.py:277
  17.9 0.0 collective-permute-done.3.st1
  17.9 3.6 %shard_map.74 = (bf16[384,128]{1,0:T(8,128)(2,1)S(1)}, f32[128,128]{1,0:T(8,128)S(1)}, f32[256,128]{1,0:T(8,128)S(1)}) custom-call(s32[16,2]{1,0:T(8,128)S(1)} %copy.9.pairs_ref, f32[8,40,128]{2,1,0:T(8,128)S(1)} %constant_dynamic-update-slice_fusion.st0, f32[8,40,128]{2,1,0:T(8,128)S(1)} %collective-permute-done.3.st1, ...), custom_call_target="tpu_custom_call" | custom-call | flops 2097152000 | tf_op jit(solution)/shard_map/pallas_call | solution.py:212
  21.5 0.0 collective-permute-done.6.so_ref
  21.6 1.5 %collective-permute-start.7 = (f32[8,8,1024]{2,1,0:T(8,128)S(1)}, f32[8,8,1024]{2,1,0:T(8,128)S(1)}, u32[]{:S(2)}, u32[]{:S(2)}) collective-permute-start(f32[8,8,1024]{2,1,0:T(8,128)S(1)} %pad_maximum_fusion), channel_id=1, source_target_pairs={{0,1},{1,0},{2,3},{3,2},{4,5},{5,4},{6,7},{7,6},{8,9},{9,8},{10,11... | collective-permute-start | bytes 786440 | tf_op jit(solution)/shard_map/ppermute | solution.py:277
  23.1 3.3 %shard_map.75.before = f32[256,128]{1,0:T(8,128)S(1)} custom-call(bf16[384,128]{1,0:T(8,128)(2,1)S(1)} %get-tuple-element.16.lhs, f32[128,128]{1,0:T(8,128)S(1)} %get-tuple-element.17.sizes, f32[256,128]{1,0:T(8,128)S(1)} %get-tuple-element.18.before, f32[4,8,1024]{2,1,0:T(8,128)S(1)} %collective-permute-done.6.so_ref), custom_call_target="tpu_custom_call" | custom-call | flops 2097152000 | tf_op jit(solution)/shard_map/pallas_call | solution.py:212
  26.4 0.0 collective-permute-done.7.so_ref
  26.4 7.0 %shard_map.76 = f32[4,2,1024]{2,1,0:T(2,128)} custom-call(s32[16,2]{1,0:T(8,128)S(1)} %copy.9.pairs_ref, bf16[384,128]{1,0:T(8,128)(2,1)S(1)} %get-tuple-element.16.lhs, f32[128,128]{1,0:T(8,128)S(1)} %get-tuple-element.17.sizes, f32[256,128]{1,0:T(8,128)S(1)} %shard_map.75.before, f32[8,8,1024]{2,1,0:T(8,128)S(1)} %collective-permute-done.7.so_ref), custom_call_target="tpu_custom_call" | custom-call | flops 4194304000 | tf_op jit(solution)/shard_map/pallas_call | solution.py:212
  (14 shorter events, 0.1 us)
Async XLA Ops:
  1.5 4.8 %collective-permute-start = (f32[1,40,128]{2,1,0:T(8,128)}, f32[1,40,128]{2,1,0:T(8,128)S(1)}, u32[]{:S(2)}, u32[]{:S(2)}) collective-permute-start(f32[1,40,128]{2,1,0:T(8,128)} %get-tuple-element.13), channel_id=1, source_target_pairs={{0,8},{1,9},{2,10},{3,11},{4,12},{5,13},{6,14},{7,15},{8,0},{9,1},... | collective-permute-start | bytes 61448 | tf_op jit(solution)/shard_map/ppermute | solution.py:277
  4.7 0.9 %copy-start = (f32[1,40,128]{2,1,0:T(8,128)S(1)}, f32[1,40,128]{2,1,0:T(8,128)}, u32[]{:S(2)}) copy-start(f32[1,40,128]{2,1,0:T(8,128)} %get-tuple-element.13) | copy-start | bytes 61444
  4.7 3.9 %collective-permute-start.4 = (f32[1,8,1024]{2,1,0:T(8,128)}, f32[1,8,1024]{2,1,0:T(8,128)S(1)}, u32[]{:S(2)}, u32[]{:S(2)}) collective-permute-start(f32[1,8,1024]{2,1,0:T(8,128)} %get-tuple-element.14), channel_id=1, source_target_pairs={{0,8},{1,9},{2,10},{3,11},{4,12},{5,13},{6,14},{7,15},{8,0},{9,1},... | collective-permute-start | bytes 98312 | tf_op jit(solution)/shard_map/ppermute | solution.py:277
  5.6 0.7 %copy-start.2 = (s32[16,2]{0,1:T(2,128)S(1)}, s32[16,2]{0,1:T(2,128)}, u32[]{:S(2)}) copy-start(s32[16,2]{0,1:T(2,128)} %param.13) | copy-start | bytes 388
  6.3 2.3 %copy-start.1 = (f32[1,8,1024]{2,1,0:T(8,128)S(1)}, f32[1,8,1024]{2,1,0:T(8,128)}, u32[]{:S(2)}) copy-start(f32[1,8,1024]{2,1,0:T(8,128)} %get-tuple-element.14) | copy-start | bytes 98308
  6.3 2.9 %collective-permute-start.1 = (f32[2,40,128]{2,1,0:T(8,128)S(1)}, f32[2,40,128]{2,1,0:T(8,128)S(1)}, u32[]{:S(2)}, u32[]{:S(2)}) collective-permute-start(f32[2,40,128]{2,1,0:T(8,128)S(1)} %pad_maximum_fusion.3), channel_id=1, source_target_pairs={{0,2},{1,3},{2,0},{3,1},{4,6},{5,7},{6,4},{7,5},{8,10},{9,11},{10,... | collective-permute-start | bytes 122888 | tf_op jit(solution)/shard_map/ppermute | solution.py:277
  9.3 3.3 %collective-permute-start.2 = (f32[4,40,128]{2,1,0:T(8,128)S(1)}, f32[4,40,128]{2,1,0:T(8,128)S(1)}, u32[]{:S(2)}, u32[]{:S(2)}) collective-permute-start(f32[4,40,128]{2,1,0:T(8,128)S(1)} %pad_maximum_fusion.1), channel_id=1, source_target_pairs={{0,4},{1,5},{2,6},{3,7},{4,0},{5,1},{6,2},{7,3},{8,12},{9,13},{10,... | collective-permute-start | bytes 245768 | tf_op jit(solution)/shard_map/ppermute | solution.py:277
  10.6 5.6 %collective-permute-start.5 = (f32[2,8,1024]{2,1,0:T(8,128)S(1)}, f32[2,8,1024]{2,1,0:T(8,128)S(1)}, u32[]{:S(2)}, u32[]{:S(2)}) collective-permute-start(f32[2,8,1024]{2,1,0:T(8,128)S(1)} %pad_maximum_fusion.2), channel_id=1, source_target_pairs={{0,4},{1,5},{2,6},{3,7},{4,0},{5,1},{6,2},{7,3},{8,12},{9,13},{10,... | collective-permute-start | bytes 196616 | tf_op jit(solution)/shard_map/ppermute | solution.py:277
  12.6 5.3 %collective-permute-start.3 = (f32[8,40,128]{2,1,0:T(8,128)S(1)}, f32[8,40,128]{2,1,0:T(8,128)S(1)}, u32[]{:S(2)}, u32[]{:S(2)}) collective-permute-start(f32[8,40,128]{2,1,0:T(8,128)S(1)} %constant_dynamic-update-slice_fusion.st0), channel_id=1, source_target_pairs={{0,1},{1,0},{2,3},{3,2},{4,5},{5,4},{6,7},{7,6},{8,9},{9,8},{10,11... | collective-permute-start | bytes 491528 | tf_op jit(solution)/shard_map/ppermute | solution.py:277
  16.2 5.4 %collective-permute-start.6 = (f32[4,8,1024]{2,1,0:T(8,128)S(1)}, f32[4,8,1024]{2,1,0:T(8,128)S(1)}, u32[]{:S(2)}, u32[]{:S(2)}) collective-permute-start(f32[4,8,1024]{2,1,0:T(8,128)S(1)} %constant_dynamic-update-slice_fusion.4.so_ref), channel_id=1, source_target_pairs={{0,2},{1,3},{2,0},{3,1},{4,6},{5,7},{6,4},{7,5},{8,10},{9,11},{10,... | collective-permute-start | bytes 393224 | tf_op jit(solution)/shard_map/ppermute | solution.py:277
  21.6 4.8 %collective-permute-start.7 = (f32[8,8,1024]{2,1,0:T(8,128)S(1)}, f32[8,8,1024]{2,1,0:T(8,128)S(1)}, u32[]{:S(2)}, u32[]{:S(2)}) collective-permute-start(f32[8,8,1024]{2,1,0:T(8,128)S(1)} %pad_maximum_fusion), channel_id=1, source_target_pairs={{0,1},{1,0},{2,3},{3,2},{4,5},{5,4},{6,7},{7,6},{8,9},{9,8},{10,11... | collective-permute-start | bytes 786440 | tf_op jit(solution)/shard_map/ppermute | solution.py:277

commit v5 on v4

--- a/solution.py
+++ b/solution.py
@@ -87,16 +87,20 @@
 
 def add_sources(chans, directions, depth, so_ref, lhs, sizes, total, *work):
     both, sides = work[:2], work[2:]
-    shards, _, width = so_ref.shape
-    step = math.gcd(width, STEP)
-    per = width // step
+    shards = so_ref.shape[0]
+    tiles = so_ref.shape[1] // COORD_ROWS
+    wide = math.gcd(tiles, STEP // LANES)
+    step = wide * LANES
+    per = tiles // wide
     half = 2 * chans * TS
     last = shards * per
     ways = math.gcd(last, WAYS)
     sides[-1][...] = jnp.zeros_like(sides[-1])
 
     def part(t):
-        return so_ref[t // per, :, pl.ds(pl.multiple_of(lax.rem(t, per) * step, step), step)]
+        row = lax.rem(t, per) * (wide * COORD_ROWS)
+        rows = [pl.ds(pl.multiple_of(row + n * COORD_ROWS, COORD_ROWS), COORD_ROWS) for n in range(wide)]
+        return jnp.concatenate([so_ref[t // per, at] for at in rows], 1)
 
     def product(t, into):
         made = source_rows(part(t), directions, depth)
@@ -207,7 +211,7 @@
 
     def call(self, kernel, out_shape, scratch, args):
         vmem = pl.BlockSpec(memory_space=pltpu.VMEM)
-        sources = args[-1].shape[0] * args[-1].shape[2]
+        sources = args[-1].size // COORD_ROWS
         count = 2 * self.chans * TS * sources
         return pl.pallas_call(
             kernel,
@@ -245,10 +249,11 @@
     directions = jones_ref.shape[2]
     coords = positions_ref[...]
     l_term, m_term = coords[0:1], coords[1:2]
-    source_ref[0, 0:2] = coords
-    source_ref[0, 2:3] = jnp.sqrt(1.0 - l_term * l_term - m_term * m_term) - 1.0
-    source_ref[0, 3:4] = cluster_ref[...].astype(jnp.float32)
-    source_ref[0, 4:] = flux_ref[...] * scale
+    n_term = jnp.sqrt(1.0 - l_term * l_term - m_term * m_term) - 1.0
+    kinds = cluster_ref[...].astype(jnp.float32)
+    source = jnp.concatenate([coords, n_term, kinds, flux_ref[...] * scale], 0)
+    for n in range(coords.shape[1] // LANES):
+        source_ref[0, n * COORD_ROWS : (n + 1) * COORD_ROWS] = source[:, n * LANES : (n + 1) * LANES]
     station_ref[...] = jnp.zeros_like(station_ref)
     for c in range(chans):
         lanes = slice(c * own, (c + 1) * own)
@@ -266,7 +271,7 @@
         functools.partial(pack_kernel, scale, chans),
         out_shape=(
             jax.ShapeDtypeStruct((1, COORD_ROWS + 2 * directions, chans * own), jnp.float32),
-            jax.ShapeDtypeStruct((1, 4 + chans, positions.shape[1]), jnp.float32),
+            jax.ShapeDtypeStruct((1, positions.shape[1] // LANES * COORD_ROWS, LANES), jnp.float32),
         ),
         in_specs=[pl.BlockSpec(memory_space=pltpu.SMEM)] + [vmem] * 5,
         out_specs=(vmem, vmem),

time: 33.6 us -> 33.6 us (level)
  no operation moved by 1% of the time
where the time goes in v5:
time: 33.6 us; the launch traced here: 33.4 us
  Pallas kernels  15.4 us (46%)
  starting transfers between devices  12.8 us (38%)
  waiting for transfers between devices  3.43 us (10%)
  local copies, waits for them, and re-layouts  1.58 us (5%)
    pallas_call x3, Pallas kernels, call(): pl.pallas_call(kernel, out_shape=out_shape, in_specs=[vmem] * len(args),...  13.9 us
    ppermute x8, starting transfers between devices, swap(): return lax.ppermute(x, 'src', [(i, i ^ bit) for i in range(size)])  12.8 us
    ppermute x8, waiting for transfers between devices, swap(): return lax.ppermute(x, 'src', [(i, i ^ bit) for i in range(size)])  3.43 us
    unnamed x12, local copies, waits for them, and re-layouts  1.57 us
    pallas_call x1, Pallas kernels, pack(): pl.pallas_call(functools.partial(pack_kernel, scale, chans), out_shape=(j...  1.55 us
  transfers between devices with their start and end apart: 8, of which 3 were waited for; matrix products, arithmetic and copies ran while one was open for 3% of the time, Pallas kernels for 21%

profile of v5, /device:TPU:1, one launch (start us, length us, event | category | flops | bytes accessed | tf_op | source)
XLA Modules:
  0.0 33.4 jit_solution(16725630484949199403)
XLA Ops:
  0.0 1.5 %shard_map.73 = (f32[1,40,128]{2,1,0:T(8,128)}, f32[1,64,128]{2,1,0:T(8,128)}) custom-call(s32[4]{0:T(128)} %channel_ref.1, f32[2,1024]{1,0:T(2,128)} %positions_ref.1, f32[4,1024]{1,0:T(4,128)} %flux_ref.1, s32[1,1024]{1,0:T(1,128)} %bitcast.2, f32[4,2,16,32]{3,2,1,0:T(8,128)} %jones_ref.1, f32[3,32]{1,0:T(4,128)} %uvw_ref.1), custom_call_target="tpu_custom_call" | custom-call | tf_op jit(solution)/shard_map/pallas_call | solution.py:270
  1.5 3.1 %collective-permute-start = (f32[1,40,128]{2,1,0:T(8,128)}, f32[1,40,128]{2,1,0:T(8,128)S(1)}, u32[]{:S(2)}, u32[]{:S(2)}) collective-permute-start(f32[1,40,128]{2,1,0:T(8,128)} %get-tuple-element.13), channel_id=1, source_target_pairs={{0,8},{1,9},{2,10},{3,11},{4,12},{5,13},{6,14},{7,15},{8,0},{9,1},... | collective-permute-start | bytes 61448 | tf_op jit(solution)/shard_map/ppermute | solution.py:282
  4.7 0.1 collective-permute-start.4
  4.8 0.8 %constant_dynamic-update-slice_fusion.6 = f32[4,64,128]{2,1,0:T(8,128)S(1)} fusion(f32[1,64,128]{2,1,0:T(8,128)} %get-tuple-element.14), kind=kLoop, calls=%fused_computation.10 | loop fusion | bytes 65536
  5.6 0.0 copy-done
  5.6 0.7 %copy-done.2 = s32[16,2]{0,1:T(2,128)S(1)} copy-done((s32[16,2]{0,1:T(2,128)S(1)}, s32[16,2]{0,1:T(2,128)}, u32[]{:S(2)}) %copy-start.2) | copy-done | bytes 152
  6.2 0.1 copy.9.pairs_ref
  6.3 0.0 collective-permute-done
  6.3 1.3 %collective-permute-start.1 = (f32[2,40,128]{2,1,0:T(8,128)S(1)}, f32[2,40,128]{2,1,0:T(8,128)S(1)}, u32[]{:S(2)}, u32[]{:S(2)}) collective-permute-start(f32[2,40,128]{2,1,0:T(8,128)S(1)} %pad_maximum_fusion.3), channel_id=1, source_target_pairs={{0,2},{1,3},{2,0},{3,1},{4,6},{5,7},{6,4},{7,5},{8,10},{9,11},{10,... | collective-permute-start | bytes 122888 | tf_op jit(solution)/shard_map/ppermute | solution.py:282
  7.6 1.0 %collective-permute-done.4 = f32[1,64,128]{2,1,0:T(8,128)S(1)} collective-permute-done((f32[1,64,128]{2,1,0:T(8,128)}, f32[1,64,128]{2,1,0:T(8,128)S(1)}, u32[]{:S(2)}, u32[]{:S(2)}) %collective-permute-start.4) | collective-permute-done | bytes 32800 | tf_op jit(solution)/shard_map/ppermute | solution.py:282
  8.6 0.6 %collective-permute-done.1 = f32[2,40,128]{2,1,0:T(8,128)S(1)} collective-permute-done((f32[2,40,128]{2,1,0:T(8,128)S(1)}, f32[2,40,128]{2,1,0:T(8,128)S(1)}, u32[]{:S(2)}, u32[]{:S(2)}) %collective-permute-start.1) | collective-permute-done | bytes 40992 | tf_op jit(solution)/shard_map/ppermute | solution.py:282
  9.3 1.3 %collective-permute-start.2 = (f32[4,40,128]{2,1,0:T(8,128)S(1)}, f32[4,40,128]{2,1,0:T(8,128)S(1)}, u32[]{:S(2)}, u32[]{:S(2)}) collective-permute-start(f32[4,40,128]{2,1,0:T(8,128)S(1)} %pad_maximum_fusion.1), channel_id=1, source_target_pairs={{0,4},{1,5},{2,6},{3,7},{4,0},{5,1},{6,2},{7,3},{8,12},{9,13},{10,... | collective-permute-start | bytes 245768 | tf_op jit(solution)/shard_map/ppermute | solution.py:282
  10.6 0.2 collective-permute-start.5
  10.7 1.8 %collective-permute-done.2 = f32[4,40,128]{2,1,0:T(8,128)S(1)} collective-permute-done((f32[4,40,128]{2,1,0:T(8,128)S(1)}, f32[4,40,128]{2,1,0:T(8,128)S(1)}, u32[]{:S(2)}, u32[]{:S(2)}) %collective-permute-start.2) | collective-permute-done | bytes 81952 | tf_op jit(solution)/shard_map/ppermute | solution.py:282
  12.6 3.6 %collective-permute-start.3 = (f32[8,40,128]{2,1,0:T(8,128)S(1)}, f32[8,40,128]{2,1,0:T(8,128)S(1)}, u32[]{:S(2)}, u32[]{:S(2)}) collective-permute-start(f32[8,40,128]{2,1,0:T(8,128)S(1)} %constant_dynamic-update-slice_fusion.st0), channel_id=1, source_target_pairs={{0,1},{1,0},{2,3},{3,2},{4,5},{5,4},{6,7},{7,6},{8,9},{9,8},{10,11... | collective-permute-start | bytes 491528 | tf_op jit(solution)/shard_map/ppermute | solution.py:282
  16.2 0.0 collective-permute-done.5
  16.2 1.7 %collective-permute-start.6 = (f32[4,64,128]{2,1,0:T(8,128)S(1)}, f32[4,64,128]{2,1,0:T(8,128)S(1)}, u32[]{:S(2)}, u32[]{:S(2)}) collective-permute-start(f32[4,64,128]{2,1,0:T(8,128)S(1)} %constant_dynamic-update-slice_fusion.4.so_ref), channel_id=1, source_target_pairs={{0,2},{1,3},{2,0},{3,1},{4,6},{5,7},{6,4},{7,5},{8,10},{9,11},{10,... | collective-permute-start | bytes 393224 | tf_op jit(solution)/shard_map/ppermute | solution.py:282
  17.9 0.0 collective-permute-done.3.st1
  17.9 3.6 %shard_map.74 = (bf16[384,128]{1,0:T(8,128)(2,1)S(1)}, f32[128,128]{1,0:T(8,128)S(1)}, f32[256,128]{1,0:T(8,128)S(1)}) custom-call(s32[16,2]{1,0:T(8,128)S(1)} %copy.9.pairs_ref, f32[8,40,128]{2,1,0:T(8,128)S(1)} %constant_dynamic-update-slice_fusion.st0, f32[8,40,128]{2,1,0:T(8,128)S(1)} %collective-permute-done.3.st1, ...), custom_call_target="tpu_custom_call" | custom-call | flops 2097152000 | tf_op jit(solution)/shard_map/pallas_call | solution.py:216
  21.5 0.0 collective-permute-done.6.so_ref
  21.6 1.5 %collective-permute-start.7 = (f32[8,64,128]{2,1,0:T(8,128)S(1)}, f32[8,64,128]{2,1,0:T(8,128)S(1)}, u32[]{:S(2)}, u32[]{:S(2)}) collective-permute-start(f32[8,64,128]{2,1,0:T(8,128)S(1)} %pad_maximum_fusion), channel_id=1, source_target_pairs={{0,1},{1,0},{2,3},{3,2},{4,5},{5,4},{6,7},{7,6},{8,9},{9,8},{10,11... | collective-permute-start | bytes 786440 | tf_op jit(solution)/shard_map/ppermute | solution.py:282
  23.1 3.3 %shard_map.75.before = f32[256,128]{1,0:T(8,128)S(1)} custom-call(bf16[384,128]{1,0:T(8,128)(2,1)S(1)} %get-tuple-element.16.lhs, f32[128,128]{1,0:T(8,128)S(1)} %get-tuple-element.17.sizes, f32[256,128]{1,0:T(8,128)S(1)} %get-tuple-element.18.before, f32[4,64,128]{2,1,0:T(8,128)S(1)} %collective-permute-done.6.so_ref), custom_call_target="tpu_custom_call" | custom-call | flops 2097152000 | tf_op jit(solution)/shard_map/pallas_call | solution.py:216
  26.4 0.0 collective-permute-done.7.so_ref
  26.4 7.0 %shard_map.76 = f32[4,2,1024]{2,1,0:T(2,128)} custom-call(s32[16,2]{1,0:T(8,128)S(1)} %copy.9.pairs_ref, bf16[384,128]{1,0:T(8,128)(2,1)S(1)} %get-tuple-element.16.lhs, f32[128,128]{1,0:T(8,128)S(1)} %get-tuple-element.17.sizes, f32[256,128]{1,0:T(8,128)S(1)} %shard_map.75.before, f32[8,64,128]{2,1,0:T(8,128)S(1)} %collective-permute-done.7.so_ref), custom_call_target="tpu_custom_call" | custom-call | flops 4194304000 | tf_op jit(solution)/shard_map/pallas_call | solution.py:216
  (14 shorter events, 0.1 us)
Async XLA Ops:
  1.5 4.8 %collective-permute-start = (f32[1,40,128]{2,1,0:T(8,128)}, f32[1,40,128]{2,1,0:T(8,128)S(1)}, u32[]{:S(2)}, u32[]{:S(2)}) collective-permute-start(f32[1,40,128]{2,1,0:T(8,128)} %get-tuple-element.13), channel_id=1, source_target_pairs={{0,8},{1,9},{2,10},{3,11},{4,12},{5,13},{6,14},{7,15},{8,0},{9,1},... | collective-permute-start | bytes 61448 | tf_op jit(solution)/shard_map/ppermute | solution.py:282
  4.7 0.9 %copy-start = (f32[1,40,128]{2,1,0:T(8,128)S(1)}, f32[1,40,128]{2,1,0:T(8,128)}, u32[]{:S(2)}) copy-start(f32[1,40,128]{2,1,0:T(8,128)} %get-tuple-element.13) | copy-start | bytes 61444
  4.7 3.9 %collective-permute-start.4 = (f32[1,64,128]{2,1,0:T(8,128)}, f32[1,64,128]{2,1,0:T(8,128)S(1)}, u32[]{:S(2)}, u32[]{:S(2)}) collective-permute-start(f32[1,64,128]{2,1,0:T(8,128)} %get-tuple-element.14), channel_id=1, source_target_pairs={{0,8},{1,9},{2,10},{3,11},{4,12},{5,13},{6,14},{7,15},{8,0},{9,1},... | collective-permute-start | bytes 98312 | tf_op jit(solution)/shard_map/ppermute | solution.py:282
  5.6 0.7 %copy-start.2 = (s32[16,2]{0,1:T(2,128)S(1)}, s32[16,2]{0,1:T(2,128)}, u32[]{:S(2)}) copy-start(s32[16,2]{0,1:T(2,128)} %param.13) | copy-start | bytes 388
  6.3 2.3 %copy-start.1 = (f32[1,64,128]{2,1,0:T(8,128)S(1)}, f32[1,64,128]{2,1,0:T(8,128)}, u32[]{:S(2)}) copy-start(f32[1,64,128]{2,1,0:T(8,128)} %get-tuple-element.14) | copy-start | bytes 98308
  6.3 2.9 %collective-permute-start.1 = (f32[2,40,128]{2,1,0:T(8,128)S(1)}, f32[2,40,128]{2,1,0:T(8,128)S(1)}, u32[]{:S(2)}, u32[]{:S(2)}) collective-permute-start(f32[2,40,128]{2,1,0:T(8,128)S(1)} %pad_maximum_fusion.3), channel_id=1, source_target_pairs={{0,2},{1,3},{2,0},{3,1},{4,6},{5,7},{6,4},{7,5},{8,10},{9,11},{10,... | collective-permute-start | bytes 122888 | tf_op jit(solution)/shard_map/ppermute | solution.py:282
  9.3 3.3 %collective-permute-start.2 = (f32[4,40,128]{2,1,0:T(8,128)S(1)}, f32[4,40,128]{2,1,0:T(8,128)S(1)}, u32[]{:S(2)}, u32[]{:S(2)}) collective-permute-start(f32[4,40,128]{2,1,0:T(8,128)S(1)} %pad_maximum_fusion.1), channel_id=1, source_target_pairs={{0,4},{1,5},{2,6},{3,7},{4,0},{5,1},{6,2},{7,3},{8,12},{9,13},{10,... | collective-permute-start | bytes 245768 | tf_op jit(solution)/shard_map/ppermute | solution.py:282
  10.6 5.6 %collective-permute-start.5 = (f32[2,64,128]{2,1,0:T(8,128)S(1)}, f32[2,64,128]{2,1,0:T(8,128)S(1)}, u32[]{:S(2)}, u32[]{:S(2)}) collective-permute-start(f32[2,64,128]{2,1,0:T(8,128)S(1)} %pad_maximum_fusion.2), channel_id=1, source_target_pairs={{0,4},{1,5},{2,6},{3,7},{4,0},{5,1},{6,2},{7,3},{8,12},{9,13},{10,... | collective-permute-start | bytes 196616 | tf_op jit(solution)/shard_map/ppermute | solution.py:282
  12.6 5.3 %collective-permute-start.3 = (f32[8,40,128]{2,1,0:T(8,128)S(1)}, f32[8,40,128]{2,1,0:T(8,128)S(1)}, u32[]{:S(2)}, u32[]{:S(2)}) collective-permute-start(f32[8,40,128]{2,1,0:T(8,128)S(1)} %constant_dynamic-update-slice_fusion.st0), channel_id=1, source_target_pairs={{0,1},{1,0},{2,3},{3,2},{4,5},{5,4},{6,7},{7,6},{8,9},{9,8},{10,11... | collective-permute-start | bytes 491528 | tf_op jit(solution)/shard_map/ppermute | solution.py:282
  16.2 5.4 %collective-permute-start.6 = (f32[4,64,128]{2,1,0:T(8,128)S(1)}, f32[4,64,128]{2,1,0:T(8,128)S(1)}, u32[]{:S(2)}, u32[]{:S(2)}) collective-permute-start(f32[4,64,128]{2,1,0:T(8,128)S(1)} %constant_dynamic-update-slice_fusion.4.so_ref), channel_id=1, source_target_pairs={{0,2},{1,3},{2,0},{3,1},{4,6},{5,7},{6,4},{7,5},{8,10},{9,11},{10,... | collective-permute-start | bytes 393224 | tf_op jit(solution)/shard_map/ppermute | solution.py:282
  21.6 4.8 %collective-permute-start.7 = (f32[8,64,128]{2,1,0:T(8,128)S(1)}, f32[8,64,128]{2,1,0:T(8,128)S(1)}, u32[]{:S(2)}, u32[]{:S(2)}) collective-permute-start(f32[8,64,128]{2,1,0:T(8,128)S(1)} %pad_maximum_fusion), channel_id=1, source_target_pairs={{0,1},{1,0},{2,3},{3,2},{4,5},{5,4},{6,7},{7,6},{8,9},{9,8},{10,11... | collective-permute-start | bytes 786440 | tf_op jit(solution)/shard_map/ppermute | solution.py:282

commit v6 on v5

--- a/solution.py
+++ b/solution.py
@@ -69,15 +69,11 @@
     return size * (0.5 * TOP - q), (size * s) * c
 
 
-def steps(size):
-    high = [1 << n for n in range(size.bit_length() - 2, 1, -1)]
-    return high[:1] + [2] + high[1:] + [1]
-
-
 def place(mask, size):
+    bits = size.bit_length() - 1
     at = 0 * mask
-    for order, bit in enumerate(steps(size)):
-        at = at | (((mask >> (bit.bit_length() - 1)) & 1) << order)
+    for order in range(bits):
+        at = at | (((mask >> (bits - 1 - order)) & 1) << order)
     return at
 
 
@@ -287,15 +283,21 @@
 
 
 def spread(station, source, size):
-    arrived = None
-    for bit in steps(size):
+    bit, arrived = size // 2, None
+    while bit > 4:
         ready = source if arrived is None else after(source, arrived)
         arrived = swap(station, bit, size)
-        if bit > 2:
-            source = jnp.concatenate([source, swap(ready, bit, size)], 0)
-        if bit > 1:
-            station = jnp.concatenate([station, arrived], 0)
-    return (station, arrived), source, swap(after(source, station), 2, size)
+        source = jnp.concatenate([source, swap(ready, bit, size)], 0)
+        station = jnp.concatenate([station, arrived], 0)
+        bit //= 2
+    arrived = swap(station, 4, size)
+    station = jnp.concatenate([station, arrived], 0)
+    ready = after(source, arrived)
+    station = jnp.concatenate([station, swap(station, 2, size)], 0)
+    across = swap(ready, 2, size)
+    other = swap(ready, 4, size)
+    across = jnp.concatenate([across, swap(other, 2, size)], 0)
+    return (station, swap(station, 1, size)), jnp.concatenate([source, other], 0), across
 
 
 def on_device(positions, flux, cluster, jones, station_uvw, channels, tile_map):

time: 33.6 us -> 33.1 us (0.985)
  waiting for transfers between devices: 3.43 us -> 2.31 us
  starting transfers between devices: 12.8 us -> 13.4 us
    ppermute x8 -> x9, waiting for transfers between devices: 3.43 us -> 2.31 us  [swap(): return lax.ppermute(x, 'src', [(i, i ^ bit) for i in range(size)])]
    ppermute x8 -> x9, starting transfers between devices: 12.8 us -> 13.4 us  [swap(): return lax.ppermute(x, 'src', [(i, i ^ bit) for i in range(size)])]
  transfers between devices with their start and end apart: 8 -> 9, of which waited for: 3 -> 3; matrix products, arithmetic and copies ran while one was open for 3% -> 3% of each run, Pallas kernels for 21% -> 21%
where the time goes in v6:
time: 33.1 us; the launch traced here: 32.8 us
  Pallas kernels  15.4 us (47%)
  starting transfers between devices  13.4 us (40%)
  waiting for transfers between devices  2.31 us (7%)
  local copies, waits for them, and re-layouts  1.58 us (5%)
    pallas_call x3, Pallas kernels, call(): pl.pallas_call(kernel, out_shape=out_shape, in_specs=[vmem] * len(args),...  13.9 us
    ppermute x9, starting transfers between devices, swap(): return lax.ppermute(x, 'src', [(i, i ^ bit) for i in range(size)])  13.4 us
    ppermute x9, waiting for transfers between devices, swap(): return lax.ppermute(x, 'src', [(i, i ^ bit) for i in range(size)])  2.31 us
    unnamed x12, local copies, waits for them, and re-layouts  1.57 us
    pallas_call x1, Pallas kernels, pack(): pl.pallas_call(functools.partial(pack_kernel, scale, chans), out_shape=(j...  1.56 us
  transfers between devices with their start and end apart: 9, of which 3 were waited for; matrix products, arithmetic and copies ran while one was open for 3% of the time, Pallas kernels for 21%

profile of v6, /device:TPU:1, one launch (start us, length us, event | category | flops | bytes accessed | tf_op | source)
XLA Modules:
  0.0 32.8 jit_solution(10413563051287704308)
XLA Ops:
  0.0 1.6 %shard_map.73 = (f32[1,40,128]{2,1,0:T(8,128)}, f32[1,64,128]{2,1,0:T(8,128)}) custom-call(s32[4]{0:T(128)} %channel_ref.1, f32[2,1024]{1,0:T(2,128)} %positions_ref.1, f32[4,1024]{1,0:T(4,128)} %flux_ref.1, s32[1,1024]{1,0:T(1,128)} %bitcast.2, f32[4,2,16,32]{3,2,1,0:T(8,128)} %jones_ref.1, f32[3,32]{1,0:T(4,128)} %uvw_ref.1), custom_call_target="tpu_custom_call" | custom-call | tf_op jit(solution)/shard_map/pallas_call | solution.py:266
  1.6 3.1 %collective-permute-start = (f32[1,40,128]{2,1,0:T(8,128)}, f32[1,40,128]{2,1,0:T(8,128)S(1)}, u32[]{:S(2)}, u32[]{:S(2)}) collective-permute-start(f32[1,40,128]{2,1,0:T(8,128)} %get-tuple-element.12), channel_id=1, source_target_pairs={{0,8},{1,9},{2,10},{3,11},{4,12},{5,13},{6,14},{7,15},{8,0},{9,1},... | collective-permute-start | bytes 61448 | tf_op jit(solution)/shard_map/ppermute | solution.py:278
  4.7 0.1 collective-permute-start.4
  4.8 0.8 %constant_dynamic-update-slice_fusion.6 = f32[4,64,128]{2,1,0:T(8,128)S(1)} fusion(f32[1,64,128]{2,1,0:T(8,128)} %get-tuple-element.13), kind=kLoop, calls=%fused_computation.11 | loop fusion | bytes 65536
  5.6 0.7 %copy-done.2 = s32[16,2]{0,1:T(2,128)S(1)} copy-done((s32[16,2]{0,1:T(2,128)S(1)}, s32[16,2]{0,1:T(2,128)}, u32[]{:S(2)}) %copy-start.2) | copy-done | bytes 152
  6.2 0.1 copy.9.pairs_ref
  6.3 0.0 collective-permute-done
  6.3 1.4 %collective-permute-start.1 = (f32[2,40,128]{2,1,0:T(8,128)S(1)}, f32[2,40,128]{2,1,0:T(8,128)S(1)}, u32[]{:S(2)}, u32[]{:S(2)}) collective-permute-start(f32[2,40,128]{2,1,0:T(8,128)S(1)} %pad_maximum_fusion.4), channel_id=1, source_target_pairs={{0,4},{1,5},{2,6},{3,7},{4,0},{5,1},{6,2},{7,3},{8,12},{9,13},{10,... | collective-permute-start | bytes 122888 | tf_op jit(solution)/shard_map/ppermute | solution.py:278
  7.7 0.9 %collective-permute-done.4 = f32[1,64,128]{2,1,0:T(8,128)S(1)} collective-permute-done((f32[1,64,128]{2,1,0:T(8,128)}, f32[1,64,128]{2,1,0:T(8,128)S(1)}, u32[]{:S(2)}, u32[]{:S(2)}) %collective-permute-start.4) | collective-permute-done | bytes 32800 | tf_op jit(solution)/shard_map/ppermute | solution.py:278
  8.6 0.6 %collective-permute-done.1 = f32[2,40,128]{2,1,0:T(8,128)S(1)} collective-permute-done((f32[2,40,128]{2,1,0:T(8,128)S(1)}, f32[2,40,128]{2,1,0:T(8,128)S(1)}, u32[]{:S(2)}, u32[]{:S(2)}) %collective-permute-start.1) | collective-permute-done | bytes 40992 | tf_op jit(solution)/shard_map/ppermute | solution.py:278
  9.3 1.2 %collective-permute-start.2 = (f32[4,40,128]{2,1,0:T(8,128)S(1)}, f32[4,40,128]{2,1,0:T(8,128)S(1)}, u32[]{:S(2)}, u32[]{:S(2)}) collective-permute-start(f32[4,40,128]{2,1,0:T(8,128)S(1)} %pad_maximum_fusion.2), channel_id=1, source_target_pairs={{0,2},{1,3},{2,0},{3,1},{4,6},{5,7},{6,4},{7,5},{8,10},{9,11},{10,... | collective-permute-start | bytes 245768 | tf_op jit(solution)/shard_map/ppermute | solution.py:278
  10.5 1.3 %collective-permute-start.5 = (f32[2,64,128]{2,1,0:T(8,128)S(1)}, f32[2,64,128]{2,1,0:T(8,128)S(1)}, u32[]{:S(2)}, u32[]{:S(2)}) collective-permute-start(f32[2,64,128]{2,1,0:T(8,128)S(1)} %pad_maximum_fusion.3), channel_id=1, source_target_pairs={{0,4},{1,5},{2,6},{3,7},{4,0},{5,1},{6,2},{7,3},{8,12},{9,13},{10,... | collective-permute-start | bytes 196616 | tf_op jit(solution)/shard_map/ppermute | solution.py:278
  11.8 0.8 %collective-permute-done.2 = f32[4,40,128]{2,1,0:T(8,128)S(1)} collective-permute-done((f32[4,40,128]{2,1,0:T(8,128)S(1)}, f32[4,40,128]{2,1,0:T(8,128)S(1)}, u32[]{:S(2)}, u32[]{:S(2)}) %collective-permute-start.2) | collective-permute-done | bytes 81952 | tf_op jit(solution)/shard_map/ppermute | solution.py:278
  12.6 3.6 %collective-permute-start.3 = (f32[8,40,128]{2,1,0:T(8,128)S(1)}, f32[8,40,128]{2,1,0:T(8,128)S(1)}, u32[]{:S(2)}, u32[]{:S(2)}) collective-permute-start(f32[8,40,128]{2,1,0:T(8,128)S(1)} %constant_dynamic-update-slice_fusion.st0), channel_id=1, source_target_pairs={{0,1},{1,0},{2,3},{3,2},{4,5},{5,4},{6,7},{7,6},{8,9},{9,8},{10,11... | collective-permute-start | bytes 491528 | tf_op jit(solution)/shard_map/ppermute | solution.py:278
  16.2 1.7 %collective-permute-start.6 = (f32[2,64,128]{2,1,0:T(8,128)S(1)}, f32[2,64,128]{2,1,0:T(8,128)S(1)}, u32[]{:S(2)}, u32[]{:S(2)}) collective-permute-start(f32[2,64,128]{2,1,0:T(8,128)S(1)} %pad_maximum_fusion.3), channel_id=1, source_target_pairs={{0,2},{1,3},{2,0},{3,1},{4,6},{5,7},{6,4},{7,5},{8,10},{9,11},{10,... | collective-permute-start | bytes 196616 | tf_op jit(solution)/shard_map/ppermute | solution.py:278
  17.8 0.0 collective-permute-done.5
  17.8 0.1 collective-permute-start.7
  17.9 0.0 collective-permute-done.3.st1
  17.9 3.6 %shard_map.74 = (bf16[384,128]{1,0:T(8,128)(2,1)S(1)}, f32[128,128]{1,0:T(8,128)S(1)}, f32[256,128]{1,0:T(8,128)S(1)}) custom-call(s32[16,2]{1,0:T(8,128)S(1)} %copy.9.pairs_ref, f32[8,40,128]{2,1,0:T(8,128)S(1)} %constant_dynamic-update-slice_fusion.st0, f32[8,40,128]{2,1,0:T(8,128)S(1)} %collective-permute-done.3.st1, ...), custom_call_target="tpu_custom_call" | custom-call | flops 2097152000 | tf_op jit(solution)/shard_map/pallas_call | solution.py:212
  21.6 0.0 collective-permute-done.6
  21.6 0.0 collective-permute-done.7
  21.6 0.9 %collective-permute-start.8 = (f32[8,64,128]{2,1,0:T(8,128)S(1)}, f32[8,64,128]{2,1,0:T(8,128)S(1)}, u32[]{:S(2)}, u32[]{:S(2)}) collective-permute-start(f32[8,64,128]{2,1,0:T(8,128)S(1)} %pad_maximum_fusion), channel_id=1, source_target_pairs={{0,1},{1,0},{2,3},{3,2},{4,5},{5,4},{6,7},{7,6},{8,9},{9,8},{10,11... | collective-permute-start | bytes 786440 | tf_op jit(solution)/shard_map/ppermute | solution.py:278
  22.6 3.3 %shard_map.75.before = f32[256,128]{1,0:T(8,128)S(1)} custom-call(bf16[384,128]{1,0:T(8,128)(2,1)S(1)} %get-tuple-element.15.lhs, f32[128,128]{1,0:T(8,128)S(1)} %get-tuple-element.16.sizes, f32[256,128]{1,0:T(8,128)S(1)} %get-tuple-element.17.before, f32[4,64,128]{2,1,0:T(8,128)S(1)} %pad_maximum_fusion.1.so_ref), custom_call_target="tpu_custom_call" | custom-call | flops 2097152000 | tf_op jit(solution)/shard_map/pallas_call | solution.py:212
  25.9 7.0 %shard_map.76 = f32[4,2,1024]{2,1,0:T(2,128)} custom-call(s32[16,2]{1,0:T(8,128)S(1)} %copy.9.pairs_ref, bf16[384,128]{1,0:T(8,128)(2,1)S(1)} %get-tuple-element.15.lhs, f32[128,128]{1,0:T(8,128)S(1)} %get-tuple-element.16.sizes, f32[256,128]{1,0:T(8,128)S(1)} %shard_map.75.before, f32[8,64,128]{2,1,0:T(8,128)S(1)} %collective-permute-done.8.so_ref), custom_call_target="tpu_custom_call" | custom-call | flops 4194304000 | tf_op jit(solution)/shard_map/pallas_call | solution.py:212
  (17 shorter events, 0.1 us)
Async XLA Ops:
  1.6 4.8 %collective-permute-start = (f32[1,40,128]{2,1,0:T(8,128)}, f32[1,40,128]{2,1,0:T(8,128)S(1)}, u32[]{:S(2)}, u32[]{:S(2)}) collective-permute-start(f32[1,40,128]{2,1,0:T(8,128)} %get-tuple-element.12), channel_id=1, source_target_pairs={{0,8},{1,9},{2,10},{3,11},{4,12},{5,13},{6,14},{7,15},{8,0},{9,1},... | collective-permute-start | bytes 61448 | tf_op jit(solution)/shard_map/ppermute | solution.py:278
  4.7 0.9 %copy-start = (f32[1,40,128]{2,1,0:T(8,128)S(1)}, f32[1,40,128]{2,1,0:T(8,128)}, u32[]{:S(2)}) copy-start(f32[1,40,128]{2,1,0:T(8,128)} %get-tuple-element.12) | copy-start | bytes 61444
  4.7 3.9 %collective-permute-start.4 = (f32[1,64,128]{2,1,0:T(8,128)}, f32[1,64,128]{2,1,0:T(8,128)S(1)}, u32[]{:S(2)}, u32[]{:S(2)}) collective-permute-start(f32[1,64,128]{2,1,0:T(8,128)} %get-tuple-element.13), channel_id=1, source_target_pairs={{0,8},{1,9},{2,10},{3,11},{4,12},{5,13},{6,14},{7,15},{8,0},{9,1},... | collective-permute-start | bytes 98312 | tf_op jit(solution)/shard_map/ppermute | solution.py:278
  5.6 0.7 %copy-start.2 = (s32[16,2]{0,1:T(2,128)S(1)}, s32[16,2]{0,1:T(2,128)}, u32[]{:S(2)}) copy-start(s32[16,2]{0,1:T(2,128)} %param.13) | copy-start | bytes 388
  6.3 2.3 %copy-start.1 = (f32[1,64,128]{2,1,0:T(8,128)S(1)}, f32[1,64,128]{2,1,0:T(8,128)}, u32[]{:S(2)}) copy-start(f32[1,64,128]{2,1,0:T(8,128)} %get-tuple-element.13) | copy-start | bytes 98308
  6.3 2.9 %collective-permute-start.1 = (f32[2,40,128]{2,1,0:T(8,128)S(1)}, f32[2,40,128]{2,1,0:T(8,128)S(1)}, u32[]{:S(2)}, u32[]{:S(2)}) collective-permute-start(f32[2,40,128]{2,1,0:T(8,128)S(1)} %pad_maximum_fusion.4), channel_id=1, source_target_pairs={{0,4},{1,5},{2,6},{3,7},{4,0},{5,1},{6,2},{7,3},{8,12},{9,13},{10,... | collective-permute-start | bytes 122888 | tf_op jit(solution)/shard_map/ppermute | solution.py:278
  9.3 3.3 %collective-permute-start.2 = (f32[4,40,128]{2,1,0:T(8,128)S(1)}, f32[4,40,128]{2,1,0:T(8,128)S(1)}, u32[]{:S(2)}, u32[]{:S(2)}) collective-permute-start(f32[4,40,128]{2,1,0:T(8,128)S(1)} %pad_maximum_fusion.2), channel_id=1, source_target_pairs={{0,2},{1,3},{2,0},{3,1},{4,6},{5,7},{6,4},{7,5},{8,10},{9,11},{10,... | collective-permute-start | bytes 245768 | tf_op jit(solution)/shard_map/ppermute | solution.py:278
  10.5 7.3 %collective-permute-start.5 = (f32[2,64,128]{2,1,0:T(8,128)S(1)}, f32[2,64,128]{2,1,0:T(8,128)S(1)}, u32[]{:S(2)}, u32[]{:S(2)}) collective-permute-start(f32[2,64,128]{2,1,0:T(8,128)S(1)} %pad_maximum_fusion.3), channel_id=1, source_target_pairs={{0,4},{1,5},{2,6},{3,7},{4,0},{5,1},{6,2},{7,3},{8,12},{9,13},{10,... | collective-permute-start | bytes 196616 | tf_op jit(solution)/shard_map/ppermute | solution.py:278
  12.6 5.4 %collective-permute-start.3 = (f32[8,40,128]{2,1,0:T(8,128)S(1)}, f32[8,40,128]{2,1,0:T(8,128)S(1)}, u32[]{:S(2)}, u32[]{:S(2)}) collective-permute-start(f32[8,40,128]{2,1,0:T(8,128)S(1)} %constant_dynamic-update-slice_fusion.st0), channel_id=1, source_target_pairs={{0,1},{1,0},{2,3},{3,2},{4,5},{5,4},{6,7},{7,6},{8,9},{9,8},{10,11... | collective-permute-start | bytes 491528 | tf_op jit(solution)/shard_map/ppermute | solution.py:278
  16.2 5.4 %collective-permute-start.6 = (f32[2,64,128]{2,1,0:T(8,128)S(1)}, f32[2,64,128]{2,1,0:T(8,128)S(1)}, u32[]{:S(2)}, u32[]{:S(2)}) collective-permute-start(f32[2,64,128]{2,1,0:T(8,128)S(1)} %pad_maximum_fusion.3), channel_id=1, source_target_pairs={{0,2},{1,3},{2,0},{3,1},{4,6},{5,7},{6,4},{7,5},{8,10},{9,11},{10,... | collective-permute-start | bytes 196616 | tf_op jit(solution)/shard_map/ppermute | solution.py:278
  17.8 3.7 %collective-permute-start.7 = (f32[2,64,128]{2,1,0:T(8,128)S(1)}, f32[2,64,128]{2,1,0:T(8,128)S(1)}, u32[]{:S(2)}, u32[]{:S(2)}) collective-permute-start(f32[2,64,128]{2,1,0:T(8,128)S(1)} %collective-permute-done.5), channel_id=1, source_target_pairs={{0,2},{1,3},{2,0},{3,1},{4,6},{5,7},{6,4},{7,5},{8,10},{9,11},{10,... | collective-permute-start | bytes 196616 | tf_op jit(solution)/shard_map/ppermute | solution.py:278
  21.6 4.3 %collective-permute-start.8 = (f32[8,64,128]{2,1,0:T(8,128)S(1)}, f32[8,64,128]{2,1,0:T(8,128)S(1)}, u32[]{:S(2)}, u32[]{:S(2)}) collective-permute-start(f32[8,64,128]{2,1,0:T(8,128)S(1)} %pad_maximum_fusion), channel_id=1, source_target_pairs={{0,1},{1,0},{2,3},{3,2},{4,5},{5,4},{6,7},{7,6},{8,9},{9,8},{10,11... | collective-permute-start | bytes 786440 | tf_op jit(solution)/shard_map/ppermute | solution.py:278

commit v7 on v6

--- a/solution.py
+++ b/solution.py
@@ -91,11 +91,12 @@
     half = 2 * chans * TS
     last = shards * per
     ways = math.gcd(last, WAYS)
-    sides[-1][...] = jnp.zeros_like(sides[-1])
+    if ways < last:
+        sides[-1][...] = jnp.zeros_like(sides[-1])
 
     def part(t):
-        row = lax.rem(t, per) * (wide * COORD_ROWS)
-        rows = [pl.ds(pl.multiple_of(row + n * COORD_ROWS, COORD_ROWS), COORD_ROWS) for n in range(wide)]
+        row = (t % per if isinstance(t, int) else lax.rem(t, per)) * (wide * COORD_ROWS)
+        rows = [pl.ds(row + n * COORD_ROWS if isinstance(t, int) else pl.multiple_of(row + n * COORD_ROWS, COORD_ROWS), COORD_ROWS) for n in range(wide)]
         return jnp.concatenate([so_ref[t // per, at] for at in rows], 1)
 
     def product(t, into):
@@ -135,8 +136,16 @@
             collect(sides[(way + 1) % 2])
         return carry
 
-    lax.fori_loop(0, last // ways, turn, 0)
-    collect(sides[-1])
+    if ways < last:
+        lax.fori_loop(0, last // ways, turn, 0)
+    else:
+        for at in range(last):
+            if at + 1 < last:
+                product(at + 1, both[(at + 1) % 2])
+            phasors(at, both[at % 2], sides[at % 2])
+            if at:
+                collect(sides[(at + 1) % 2])
+    collect(sides[(last - 1) % 2])
 
 
 def first_kernel(chans, directions, depth, row, size, pairs_ref, st0, st1, so_ref, lhs, sizes, total, *work):

time: 33.1 us -> 33.1 us (level)
  no operation moved by 1% of the time
where the time goes in v7:
time: 33.1 us; the launch traced here: 32.8 us
  Pallas kernels  15.4 us (47%)
  starting transfers between devices  13.4 us (40%)
  waiting for transfers between devices  2.31 us (7%)
  local copies, waits for them, and re-layouts  1.58 us (5%)
    pallas_call x3, Pallas kernels, call(): pl.pallas_call(kernel, out_shape=out_shape, in_specs=[vmem] * len(args),...  13.8 us
    ppermute x9, starting transfers between devices, swap(): return lax.ppermute(x, 'src', [(i, i ^ bit) for i in range(size)])  13.4 us
    ppermute x9, waiting for transfers between devices, swap(): return lax.ppermute(x, 'src', [(i, i ^ bit) for i in range(size)])  2.31 us
    unnamed x12, local copies, waits for them, and re-layouts  1.57 us
    pallas_call x1, Pallas kernels, pack(): pl.pallas_call(functools.partial(pack_kernel, scale, chans), out_shape=(j...  1.56 us
  transfers between devices with their start and end apart: 9, of which 3 were waited for; matrix products, arithmetic and copies ran while one was open for 3% of the time, Pallas kernels for 21%

profile of v7, /device:TPU:1, one launch (start us, length us, event | category | flops | bytes accessed | tf_op | source)
XLA Modules:
  0.0 32.8 jit_solution(6664849265305647973)
XLA Ops:
  0.0 1.6 %shard_map.73 = (f32[1,40,128]{2,1,0:T(8,128)}, f32[1,64,128]{2,1,0:T(8,128)}) custom-call(s32[4]{0:T(128)} %channel_ref.1, f32[2,1024]{1,0:T(2,128)} %positions_ref.1, f32[4,1024]{1,0:T(4,128)} %flux_ref.1, s32[1,1024]{1,0:T(1,128)} %bitcast.2, f32[4,2,16,32]{3,2,1,0:T(8,128)} %jones_ref.1, f32[3,32]{1,0:T(4,128)} %uvw_ref.1), custom_call_target="tpu_custom_call" | custom-call | tf_op jit(solution)/shard_map/pallas_call | solution.py:275
  1.6 3.1 %collective-permute-start = (f32[1,40,128]{2,1,0:T(8,128)}, f32[1,40,128]{2,1,0:T(8,128)S(1)}, u32[]{:S(2)}, u32[]{:S(2)}) collective-permute-start(f32[1,40,128]{2,1,0:T(8,128)} %get-tuple-element.12), channel_id=1, source_target_pairs={{0,8},{1,9},{2,10},{3,11},{4,12},{5,13},{6,14},{7,15},{8,0},{9,1},... | collective-permute-start | bytes 61448 | tf_op jit(solution)/shard_map/ppermute | solution.py:287
  4.7 0.1 collective-permute-start.4
  4.8 0.8 %constant_dynamic-update-slice_fusion.6 = f32[4,64,128]{2,1,0:T(8,128)S(1)} fusion(f32[1,64,128]{2,1,0:T(8,128)} %get-tuple-element.13), kind=kLoop, calls=%fused_computation.11 | loop fusion | bytes 65536
  5.6 0.7 %copy-done.2 = s32[16,2]{0,1:T(2,128)S(1)} copy-done((s32[16,2]{0,1:T(2,128)S(1)}, s32[16,2]{0,1:T(2,128)}, u32[]{:S(2)}) %copy-start.2) | copy-done | bytes 152
  6.2 0.1 copy.9.pairs_ref
  6.3 0.0 collective-permute-done
  6.3 1.4 %collective-permute-start.1 = (f32[2,40,128]{2,1,0:T(8,128)S(1)}, f32[2,40,128]{2,1,0:T(8,128)S(1)}, u32[]{:S(2)}, u32[]{:S(2)}) collective-permute-start(f32[2,40,128]{2,1,0:T(8,128)S(1)} %pad_maximum_fusion.4), channel_id=1, source_target_pairs={{0,4},{1,5},{2,6},{3,7},{4,0},{5,1},{6,2},{7,3},{8,12},{9,13},{10,... | collective-permute-start | bytes 122888 | tf_op jit(solution)/shard_map/ppermute | solution.py:287
  7.7 0.9 %collective-permute-done.4 = f32[1,64,128]{2,1,0:T(8,128)S(1)} collective-permute-done((f32[1,64,128]{2,1,0:T(8,128)}, f32[1,64,128]{2,1,0:T(8,128)S(1)}, u32[]{:S(2)}, u32[]{:S(2)}) %collective-permute-start.4) | collective-permute-done | bytes 32800 | tf_op jit(solution)/shard_map/ppermute | solution.py:287
  8.6 0.6 %collective-permute-done.1 = f32[2,40,128]{2,1,0:T(8,128)S(1)} collective-permute-done((f32[2,40,128]{2,1,0:T(8,128)S(1)}, f32[2,40,128]{2,1,0:T(8,128)S(1)}, u32[]{:S(2)}, u32[]{:S(2)}) %collective-permute-start.1) | collective-permute-done | bytes 40992 | tf_op jit(solution)/shard_map/ppermute | solution.py:287
  9.3 1.2 %collective-permute-start.2 = (f32[4,40,128]{2,1,0:T(8,128)S(1)}, f32[4,40,128]{2,1,0:T(8,128)S(1)}, u32[]{:S(2)}, u32[]{:S(2)}) collective-permute-start(f32[4,40,128]{2,1,0:T(8,128)S(1)} %pad_maximum_fusion.2), channel_id=1, source_target_pairs={{0,2},{1,3},{2,0},{3,1},{4,6},{5,7},{6,4},{7,5},{8,10},{9,11},{10,... | collective-permute-start | bytes 245768 | tf_op jit(solution)/shard_map/ppermute | solution.py:287
  10.5 1.3 %collective-permute-start.5 = (f32[2,64,128]{2,1,0:T(8,128)S(1)}, f32[2,64,128]{2,1,0:T(8,128)S(1)}, u32[]{:S(2)}, u32[]{:S(2)}) collective-permute-start(f32[2,64,128]{2,1,0:T(8,128)S(1)} %pad_maximum_fusion.3), channel_id=1, source_target_pairs={{0,4},{1,5},{2,6},{3,7},{4,0},{5,1},{6,2},{7,3},{8,12},{9,13},{10,... | collective-permute-start | bytes 196616 | tf_op jit(solution)/shard_map/ppermute | solution.py:287
  11.8 0.8 %collective-permute-done.2 = f32[4,40,128]{2,1,0:T(8,128)S(1)} collective-permute-done((f32[4,40,128]{2,1,0:T(8,128)S(1)}, f32[4,40,128]{2,1,0:T(8,128)S(1)}, u32[]{:S(2)}, u32[]{:S(2)}) %collective-permute-start.2) | collective-permute-done | bytes 81952 | tf_op jit(solution)/shard_map/ppermute | solution.py:287
  12.6 3.6 %collective-permute-start.3 = (f32[8,40,128]{2,1,0:T(8,128)S(1)}, f32[8,40,128]{2,1,0:T(8,128)S(1)}, u32[]{:S(2)}, u32[]{:S(2)}) collective-permute-start(f32[8,40,128]{2,1,0:T(8,128)S(1)} %constant_dynamic-update-slice_fusion.st0), channel_id=1, source_target_pairs={{0,1},{1,0},{2,3},{3,2},{4,5},{5,4},{6,7},{7,6},{8,9},{9,8},{10,11... | collective-permute-start | bytes 491528 | tf_op jit(solution)/shard_map/ppermute | solution.py:287
  16.2 1.7 %collective-permute-start.6 = (f32[2,64,128]{2,1,0:T(8,128)S(1)}, f32[2,64,128]{2,1,0:T(8,128)S(1)}, u32[]{:S(2)}, u32[]{:S(2)}) collective-permute-start(f32[2,64,128]{2,1,0:T(8,128)S(1)} %pad_maximum_fusion.3), channel_id=1, source_target_pairs={{0,2},{1,3},{2,0},{3,1},{4,6},{5,7},{6,4},{7,5},{8,10},{9,11},{10,... | collective-permute-start | bytes 196616 | tf_op jit(solution)/shard_map/ppermute | solution.py:287
  17.8 0.0 collective-permute-done.5
  17.8 0.1 collective-permute-start.7
  17.9 0.0 collective-permute-done.3.st1
  17.9 3.6 %shard_map.74 = (bf16[384,128]{1,0:T(8,128)(2,1)S(1)}, f32[128,128]{1,0:T(8,128)S(1)}, f32[256,128]{1,0:T(8,128)S(1)}) custom-call(s32[16,2]{1,0:T(8,128)S(1)} %copy.9.pairs_ref, f32[8,40,128]{2,1,0:T(8,128)S(1)} %constant_dynamic-update-slice_fusion.st0, f32[8,40,128]{2,1,0:T(8,128)S(1)} %collective-permute-done.3.st1, ...), custom_call_target="tpu_custom_call" | custom-call | flops 2097152000 | tf_op jit(solution)/shard_map/pallas_call | solution.py:221
  21.5 0.0 collective-permute-done.6
  21.6 1.0 %collective-permute-start.8 = (f32[8,64,128]{2,1,0:T(8,128)S(1)}, f32[8,64,128]{2,1,0:T(8,128)S(1)}, u32[]{:S(2)}, u32[]{:S(2)}) collective-permute-start(f32[8,64,128]{2,1,0:T(8,128)S(1)} %pad_maximum_fusion), channel_id=1, source_target_pairs={{0,1},{1,0},{2,3},{3,2},{4,5},{5,4},{6,7},{7,6},{8,9},{9,8},{10,11... | collective-permute-start | bytes 786440 | tf_op jit(solution)/shard_map/ppermute | solution.py:287
  22.6 3.3 %shard_map.75.before = f32[256,128]{1,0:T(8,128)S(1)} custom-call(bf16[384,128]{1,0:T(8,128)(2,1)S(1)} %get-tuple-element.15.lhs, f32[128,128]{1,0:T(8,128)S(1)} %get-tuple-element.16.sizes, f32[256,128]{1,0:T(8,128)S(1)} %get-tuple-element.17.before, f32[4,64,128]{2,1,0:T(8,128)S(1)} %pad_maximum_fusion.1.so_ref), custom_call_target="tpu_custom_call" | custom-call | flops 2097152000 | tf_op jit(solution)/shard_map/pallas_call | solution.py:221
  25.8 0.0 collective-permute-done.8.so_ref
  25.8 7.0 %shard_map.76 = f32[4,2,1024]{2,1,0:T(2,128)} custom-call(s32[16,2]{1,0:T(8,128)S(1)} %copy.9.pairs_ref, bf16[384,128]{1,0:T(8,128)(2,1)S(1)} %get-tuple-element.15.lhs, f32[128,128]{1,0:T(8,128)S(1)} %get-tuple-element.16.sizes, f32[256,128]{1,0:T(8,128)S(1)} %shard_map.75.before, f32[8,64,128]{2,1,0:T(8,128)S(1)} %collective-permute-done.8.so_ref), custom_call_target="tpu_custom_call" | custom-call | flops 4194304000 | tf_op jit(solution)/shard_map/pallas_call | solution.py:221
  (17 shorter events, 0.1 us)
Async XLA Ops:
  1.6 4.8 %collective-permute-start = (f32[1,40,128]{2,1,0:T(8,128)}, f32[1,40,128]{2,1,0:T(8,128)S(1)}, u32[]{:S(2)}, u32[]{:S(2)}) collective-permute-start(f32[1,40,128]{2,1,0:T(8,128)} %get-tuple-element.12), channel_id=1, source_target_pairs={{0,8},{1,9},{2,10},{3,11},{4,12},{5,13},{6,14},{7,15},{8,0},{9,1},... | collective-permute-start | bytes 61448 | tf_op jit(solution)/shard_map/ppermute | solution.py:287
  4.7 0.9 %copy-start = (f32[1,40,128]{2,1,0:T(8,128)S(1)}, f32[1,40,128]{2,1,0:T(8,128)}, u32[]{:S(2)}) copy-start(f32[1,40,128]{2,1,0:T(8,128)} %get-tuple-element.12) | copy-start | bytes 61444
  4.7 3.9 %collective-permute-start.4 = (f32[1,64,128]{2,1,0:T(8,128)}, f32[1,64,128]{2,1,0:T(8,128)S(1)}, u32[]{:S(2)}, u32[]{:S(2)}) collective-permute-start(f32[1,64,128]{2,1,0:T(8,128)} %get-tuple-element.13), channel_id=1, source_target_pairs={{0,8},{1,9},{2,10},{3,11},{4,12},{5,13},{6,14},{7,15},{8,0},{9,1},... | collective-permute-start | bytes 98312 | tf_op jit(solution)/shard_map/ppermute | solution.py:287
  5.6 0.7 %copy-start.2 = (s32[16,2]{0,1:T(2,128)S(1)}, s32[16,2]{0,1:T(2,128)}, u32[]{:S(2)}) copy-start(s32[16,2]{0,1:T(2,128)} %param.13) | copy-start | bytes 388
  6.3 2.3 %copy-start.1 = (f32[1,64,128]{2,1,0:T(8,128)S(1)}, f32[1,64,128]{2,1,0:T(8,128)}, u32[]{:S(2)}) copy-start(f32[1,64,128]{2,1,0:T(8,128)} %get-tuple-element.13) | copy-start | bytes 98308
  6.3 2.9 %collective-permute-start.1 = (f32[2,40,128]{2,1,0:T(8,128)S(1)}, f32[2,40,128]{2,1,0:T(8,128)S(1)}, u32[]{:S(2)}, u32[]{:S(2)}) collective-permute-start(f32[2,40,128]{2,1,0:T(8,128)S(1)} %pad_maximum_fusion.4), channel_id=1, source_target_pairs={{0,4},{1,5},{2,6},{3,7},{4,0},{5,1},{6,2},{7,3},{8,12},{9,13},{10,... | collective-permute-start | bytes 122888 | tf_op jit(solution)/shard_map/ppermute | solution.py:287
  9.3 3.3 %collective-permute-start.2 = (f32[4,40,128]{2,1,0:T(8,128)S(1)}, f32[4,40,128]{2,1,0:T(8,128)S(1)}, u32[]{:S(2)}, u32[]{:S(2)}) collective-permute-start(f32[4,40,128]{2,1,0:T(8,128)S(1)} %pad_maximum_fusion.2), channel_id=1, source_target_pairs={{0,2},{1,3},{2,0},{3,1},{4,6},{5,7},{6,4},{7,5},{8,10},{9,11},{10,... | collective-permute-start | bytes 245768 | tf_op jit(solution)/shard_map/ppermute | solution.py:287
  10.5 7.3 %collective-permute-start.5 = (f32[2,64,128]{2,1,0:T(8,128)S(1)}, f32[2,64,128]{2,1,0:T(8,128)S(1)}, u32[]{:S(2)}, u32[]{:S(2)}) collective-permute-start(f32[2,64,128]{2,1,0:T(8,128)S(1)} %pad_maximum_fusion.3), channel_id=1, source_target_pairs={{0,4},{1,5},{2,6},{3,7},{4,0},{5,1},{6,2},{7,3},{8,12},{9,13},{10,... | collective-permute-start | bytes 196616 | tf_op jit(solution)/shard_map/ppermute | solution.py:287
  12.6 5.4 %collective-permute-start.3 = (f32[8,40,128]{2,1,0:T(8,128)S(1)}, f32[8,40,128]{2,1,0:T(8,128)S(1)}, u32[]{:S(2)}, u32[]{:S(2)}) collective-permute-start(f32[8,40,128]{2,1,0:T(8,128)S(1)} %constant_dynamic-update-slice_fusion.st0), channel_id=1, source_target_pairs={{0,1},{1,0},{2,3},{3,2},{4,5},{5,4},{6,7},{7,6},{8,9},{9,8},{10,11... | collective-permute-start | bytes 491528 | tf_op jit(solution)/shard_map/ppermute | solution.py:287
  16.2 5.4 %collective-permute-start.6 = (f32[2,64,128]{2,1,0:T(8,128)S(1)}, f32[2,64,128]{2,1,0:T(8,128)S(1)}, u32[]{:S(2)}, u32[]{:S(2)}) collective-permute-start(f32[2,64,128]{2,1,0:T(8,128)S(1)} %pad_maximum_fusion.3), channel_id=1, source_target_pairs={{0,2},{1,3},{2,0},{3,1},{4,6},{5,7},{6,4},{7,5},{8,10},{9,11},{10,... | collective-permute-start | bytes 196616 | tf_op jit(solution)/shard_map/ppermute | solution.py:287
  17.8 3.7 %collective-permute-start.7 = (f32[2,64,128]{2,1,0:T(8,128)S(1)}, f32[2,64,128]{2,1,0:T(8,128)S(1)}, u32[]{:S(2)}, u32[]{:S(2)}) collective-permute-start(f32[2,64,128]{2,1,0:T(8,128)S(1)} %collective-permute-done.5), channel_id=1, source_target_pairs={{0,2},{1,3},{2,0},{3,1},{4,6},{5,7},{6,4},{7,5},{8,10},{9,11},{10,... | collective-permute-start | bytes 196616 | tf_op jit(solution)/shard_map/ppermute | solution.py:287
  21.6 4.2 %collective-permute-start.8 = (f32[8,64,128]{2,1,0:T(8,128)S(1)}, f32[8,64,128]{2,1,0:T(8,128)S(1)}, u32[]{:S(2)}, u32[]{:S(2)}) collective-permute-start(f32[8,64,128]{2,1,0:T(8,128)S(1)} %pad_maximum_fusion), channel_id=1, source_target_pairs={{0,1},{1,0},{2,3},{3,2},{4,5},{5,4},{6,7},{7,6},{8,9},{9,8},{10,11... | collective-permute-start | bytes 786440 | tf_op jit(solution)/shard_map/ppermute | solution.py:287
